TPU v7x, 32 devices: a whole 2x2x4 slice. The times are simulated.
32 devices in a mesh: seq: 16 (over z, x, core), head: 2 (over y).
Axes of the slice: x: 2, y: 2, z: 4, core: 2. Of those that a mesh axis runs over, the one named last changes fastest.
Arguments:
- queries: bfloat16 [3072, 5120], P('seq', 'head'), may hold values from -8 to 8
- cur_keys: bfloat16 [3072, 5120], P('seq', 'head'), may hold values from -8 to 8
- cur_values: bfloat16 [3072, 5120], P('seq', 'head'), may hold values from -6 to 6
- hist_keys: bfloat16 [7168, 5120], P('seq', 'head'), may hold values from -8 to 8
- hist_values: bfloat16 [7168, 5120], P('seq', 'head'), may hold values from -6 to 6
- piece_readers: int32 [224, 2], P('seq'), may hold values from 0 to 15, as said below
- out_weight: bfloat16 [5120, 5120], P('head'), may hold values from -0.3125 to 0.3125
Outputs:
- attn_out: bfloat16 [3072, 5120], P('seq', 'head')
Inputs may be any that keep to these rules, and one draw needn't show every extreme that they name: `piece_readers`: row j names 2 different reader blocks (indices of seq); piece j is held by index j // 14 of seq. One holder sends at most 2 pieces to one reader block: each holder sends to exactly 14 reader blocks, 2 pieces to each, and in every draw one reader block receives 2 pieces from every holder.
All inputs are finite; a program needn't handle non-finite values.
Results may differ from a plain program's by a relative error of at most 0.018.
Values may be sent and summed in bfloat16 or wider, within the bound.
A program may use at most 192 MiB of HBM per device.

v0:
```python
import math

import jax
import jax.numpy as jnp
from jax import lax
from jax.sharding import PartitionSpec as P

HDIM = 128
CAP = 2


def passed_along(value, axis, by):
    length = lax.axis_size(axis)
    return lax.ppermute(value, axis, [(i, (i + by) % length) for i in range(length)])


def attend(totals, query_heads, key_val, valid_keys):
    run_max, run_num, run_sum = totals
    head_count = query_heads.shape[1]
    key_heads = key_val[0].reshape(-1, head_count, HDIM)
    val_heads = key_val[1].reshape(-1, head_count, HDIM)
    scores = jnp.einsum("qhd,khd->hqk", query_heads, key_heads, preferred_element_type=jnp.float32)
    scores = scores * (1.0 / math.sqrt(HDIM))
    if valid_keys is not None:
        scores = jnp.where(valid_keys[None, None, :], scores, -1e30)
    new_max = jnp.maximum(run_max, jnp.max(scores, axis=-1))
    weights = jnp.exp(scores - new_max[..., None])
    if valid_keys is not None:
        weights = jnp.where(valid_keys[None, None, :], weights, 0.0)
    fade_by = jnp.exp(run_max - new_max)
    product = jnp.einsum(
        "hqk,khd->hqd", weights.astype(jnp.bfloat16), val_heads, preferred_element_type=jnp.float32
    )
    run_num = run_num * fade_by[..., None] + product
    run_sum = run_sum * fade_by + jnp.sum(weights, axis=-1)
    return (new_max, run_num, run_sum)


def local(queries, cur_keys, cur_values, hist_keys, hist_values, piece_readers, out_weight):
    tok_rows = queries.shape[0]
    width = queries.shape[1]
    head_count = width // HDIM
    query_heads = queries.reshape(tok_rows, head_count, HDIM)
    reader_count = lax.axis_size("seq")
    owner_rows = piece_readers.shape[0]
    piece_len = hist_keys.shape[0] // owner_rows
    reader_ids = jnp.arange(reader_count, dtype=jnp.int32)
    hits = jnp.sum(
        (piece_readers[:, :, None] == reader_ids[None, None, :]).astype(jnp.int32), axis=1
    )
    earlier = jnp.cumsum(hits, axis=0) - hits
    slot_ids = jnp.arange(CAP, dtype=jnp.int32)
    select = hits[None, :, :] * (earlier[None, :, :] == slot_ids[:, None, None]).astype(jnp.int32)
    select = jnp.transpose(select, (2, 0, 1))
    slot_full = jnp.sum(select, axis=2)[None, :, :]
    stacked = jnp.stack([hist_keys, hist_values]).reshape(2, owner_rows, piece_len * width)
    outgoing = jnp.einsum(
        "rcp,spx->srcx", select.astype(jnp.bfloat16), stacked, preferred_element_type=jnp.float32
    ).astype(jnp.bfloat16)
    arrived, arrived_full = (
        lax.all_to_all(outgoing, "seq", split_axis=1, concat_axis=1, tiled=True),
        lax.all_to_all(slot_full, "seq", split_axis=1, concat_axis=1, tiled=True),
    )
    hist_kv = arrived.reshape(2, -1, width)
    valid_keys = jnp.repeat(arrived_full.reshape(-1), piece_len) > 0
    start_totals = (
        jnp.full((head_count, tok_rows), -1e30, jnp.float32),
        jnp.zeros((head_count, tok_rows, HDIM), jnp.float32),
        jnp.zeros((head_count, tok_rows), jnp.float32),
    )
    totals = attend(start_totals, query_heads, hist_kv, valid_keys)
    own_block = jnp.stack([cur_keys, cur_values])
    totals = attend(totals, query_heads, own_block, None)

    def cycle_turn(step_idx, loop_state):
        travel, inner = loop_state
        travel = passed_along(travel, "seq", 1)
        return (travel, attend(inner, query_heads, travel, None))

    travel_end, totals = lax.fori_loop(0, reader_count - 1, cycle_turn, (own_block, totals))
    run_max, run_num, run_sum = totals
    attended = run_num / run_sum[..., None]
    attended = jnp.transpose(attended, (1, 0, 2)).reshape(tok_rows, width).astype(jnp.bfloat16)
    partial_out = jnp.dot(attended, out_weight, preferred_element_type=jnp.float32)
    return lax.psum_scatter(
        partial_out.astype(jnp.bfloat16), "head", scatter_dimension=1, tiled=True
    )


def solution(mesh):
    placed = (
        P("seq", "head"),
        P("seq", "head"),
        P("seq", "head"),
        P("seq", "head"),
        P("seq", "head"),
        P("seq", None),
        P("head", None),
    )
    return jax.shard_map(
        local, mesh=mesh, in_specs=placed, out_specs=P("seq", "head"), check_vma=False
    )
```

profile of v0, /device:TPU:0, one launch (start us, length us, event | category | flops | bytes accessed | tf_op | source)
XLA Modules:
  0.0 976.7 jit_solution(8585973926445731557)
XLA Ops:
  8.6 7.4 all-to-all-start
  15.9 3.6 stack.21
  19.5 3.7 stack.22
  23.2 5.4 fusion.12
  28.6 21.6 %copy.52 = bf16[2,16,2,81920]{3,2,0,1:T(2,128)(2,1)} copy(bf16[2,16,2,81920]{3,1,2,0:T(8,128)(2,1)S(1)} %fusion.12) | data formatting | bytes 20971520 | tf_op jit(solution)/shard_map/convert_element_type | solution.py:59
  50.2 6.2 all-to-all-start.1
  62.1 181.5 %all-to-all-done.1 = bf16[2,16,2,81920]{3,2,0,1:T(2,128)(2,1)} async-done(((bf16[2,16,2,81920]{3,2,0,1:T(2,128)(2,1)}), bf16[2,16,2,81920]{3,2,0,1:T(2,128)(2,1)}, u32[]{:S(2)}, u32[]{:S(2)}) %all-to-all-start.1) | async-done | bytes 10485792 | tf_op jit(solution)/shard_map/all_to_all | solution.py:61
  243.6 10.3 %fusion.56 = (bf16[1,16,2,81920]{3,2,0,1:T(2,128)(2,1)}, bf16[1,16,2,81920]{3,2,0,1:T(2,128)(2,1)}) fusion(bf16[2,16,2,81920]{3,2,0,1:T(2,128)(2,1)} %all-to-all-done.1), kind=kLoop, calls=%fused_computation.75 | loop fusion | bytes 20971520 | tf_op jit(solution)/shard_map/slice | solution.py:21
  254.0 12.4 %reshape_squeeze.6 = bf16[1024,20,128]{2,1,0:T(8,128)(2,1)} reshape(bf16[1,16,2,81920]{3,2,0,1:T(2,128)(2,1)} %get-tuple-element.79) | data formatting | bytes 10485760 | tf_op jit(solution)/shard_map/reshape;squeeze | solution.py:20
  266.3 12.4 %reshape_squeeze.7 = bf16[1024,20,128]{2,1,0:T(8,128)(2,1)} reshape(bf16[1,16,2,81920]{3,2,0,1:T(2,128)(2,1)} %get-tuple-element.78) | data formatting | bytes 10485760 | tf_op jit(solution)/shard_map/reshape;squeeze | solution.py:21
  278.8 11.0 %bitcast_reduce_fusion = (f32[20,192]{1,0:T(8,128)S(1)}, f32[20,1024,192]{1,2,0:T(8,128)}) fusion(pred[1024]{0:T(1024)(128)(4,1)S(1)} %gt.20, bf16[1024,20,128]{2,1,0:T(8,128)(2,1)} %reshape_squeeze.6, bf16[192,2560]{1,0:T(8,128)(2,1)S(1)} %copy-done), kind=kOutput, calls=%fused_computation.17 | convolution fusion | flops 1018425600 | bytes 21970944 | tf_op jit(solution)/shard_map/qhd,khd->hqk/dot_general | solution.py:22
  289.8 8.9 fusion.15
  299.9 9.2 fusion.17
  310.7 3.2 multiply_add_fusion.2
  313.9 612.4 %while.16 = (s32[]{:T(128)}, bf16[2,192,2560]{2,1,0:T(8,128)(2,1)}, f32[20,192]{1,0:T(8,128)S(1)}, f32[20,192,128]{2,1,0:T(8,128)}, f32[20,192]{1,0:T(8,128)S(1)}, /*index=5*/bf16[192,20,128]{2,0,1:T(8,128)(2,1)}, s32[]{:T(128)}) while((s32[]{:T(128)}, bf16[2,192,2560]{2,1,0:T(8,128)(2,1)}, f32[20,192]{1,0:T(8,128)S(1)}, ...), condition=%wide.region_10.11_spmd, body=%wide.region_7.10_spmd.sunk | while | flops 384376320 | bytes 51364012 | solution.py:80
  314.7 65.2 %collective-permute-done = bf16[2,192,2560]{2,1,0:T(8,128)(2,1)S(1)} collective-permute-done((bf16[2,192,2560]{2,1,0:T(8,128)(2,1)}, bf16[2,192,2560]{2,1,0:T(8,128)(2,1)S(1)}, u32[]{:S(2)}, u32[]{:S(2)}) %collective-permute-start) | collective-permute-done | bytes 1966112 | tf_op jit(solution)/shard_map/while/body/eval_jaxpr/ppermute | solution.py:14
  391.1 27.0 %collective-permute-done = bf16[2,192,2560]{2,1,0:T(8,128)(2,1)S(1)} collective-permute-done((bf16[2,192,2560]{2,1,0:T(8,128)(2,1)}, bf16[2,192,2560]{2,1,0:T(8,128)(2,1)S(1)}, u32[]{:S(2)}, u32[]{:S(2)}) %collective-permute-start) | collective-permute-done | bytes 1966112 | tf_op jit(solution)/shard_map/while/body/eval_jaxpr/ppermute | solution.py:14
  429.3 27.0 %collective-permute-done = bf16[2,192,2560]{2,1,0:T(8,128)(2,1)S(1)} collective-permute-done((bf16[2,192,2560]{2,1,0:T(8,128)(2,1)}, bf16[2,192,2560]{2,1,0:T(8,128)(2,1)S(1)}, u32[]{:S(2)}, u32[]{:S(2)}) %collective-permute-start) | collective-permute-done | bytes 1966112 | tf_op jit(solution)/shard_map/while/body/eval_jaxpr/ppermute | solution.py:14
  467.6 27.0 %collective-permute-done = bf16[2,192,2560]{2,1,0:T(8,128)(2,1)S(1)} collective-permute-done((bf16[2,192,2560]{2,1,0:T(8,128)(2,1)}, bf16[2,192,2560]{2,1,0:T(8,128)(2,1)S(1)}, u32[]{:S(2)}, u32[]{:S(2)}) %collective-permute-start) | collective-permute-done | bytes 1966112 | tf_op jit(solution)/shard_map/while/body/eval_jaxpr/ppermute | solution.py:14
  505.8 27.0 %collective-permute-done = bf16[2,192,2560]{2,1,0:T(8,128)(2,1)S(1)} collective-permute-done((bf16[2,192,2560]{2,1,0:T(8,128)(2,1)}, bf16[2,192,2560]{2,1,0:T(8,128)(2,1)S(1)}, u32[]{:S(2)}, u32[]{:S(2)}) %collective-permute-start) | collective-permute-done | bytes 1966112 | tf_op jit(solution)/shard_map/while/body/eval_jaxpr/ppermute | solution.py:14
  544.0 27.0 %collective-permute-done = bf16[2,192,2560]{2,1,0:T(8,128)(2,1)S(1)} collective-permute-done((bf16[2,192,2560]{2,1,0:T(8,128)(2,1)}, bf16[2,192,2560]{2,1,0:T(8,128)(2,1)S(1)}, u32[]{:S(2)}, u32[]{:S(2)}) %collective-permute-start) | collective-permute-done | bytes 1966112 | tf_op jit(solution)/shard_map/while/body/eval_jaxpr/ppermute | solution.py:14
  582.2 27.0 %collective-permute-done = bf16[2,192,2560]{2,1,0:T(8,128)(2,1)S(1)} collective-permute-done((bf16[2,192,2560]{2,1,0:T(8,128)(2,1)}, bf16[2,192,2560]{2,1,0:T(8,128)(2,1)S(1)}, u32[]{:S(2)}, u32[]{:S(2)}) %collective-permute-start) | collective-permute-done | bytes 1966112 | tf_op jit(solution)/shard_map/while/body/eval_jaxpr/ppermute | solution.py:14
  620.5 27.0 %collective-permute-done = bf16[2,192,2560]{2,1,0:T(8,128)(2,1)S(1)} collective-permute-done((bf16[2,192,2560]{2,1,0:T(8,128)(2,1)}, bf16[2,192,2560]{2,1,0:T(8,128)(2,1)S(1)}, u32[]{:S(2)}, u32[]{:S(2)}) %collective-permute-start) | collective-permute-done | bytes 1966112 | tf_op jit(solution)/shard_map/while/body/eval_jaxpr/ppermute | solution.py:14
  658.7 27.0 %collective-permute-done = bf16[2,192,2560]{2,1,0:T(8,128)(2,1)S(1)} collective-permute-done((bf16[2,192,2560]{2,1,0:T(8,128)(2,1)}, bf16[2,192,2560]{2,1,0:T(8,128)(2,1)S(1)}, u32[]{:S(2)}, u32[]{:S(2)}) %collective-permute-start) | collective-permute-done | bytes 1966112 | tf_op jit(solution)/shard_map/while/body/eval_jaxpr/ppermute | solution.py:14
  696.9 27.0 %collective-permute-done = bf16[2,192,2560]{2,1,0:T(8,128)(2,1)S(1)} collective-permute-done((bf16[2,192,2560]{2,1,0:T(8,128)(2,1)}, bf16[2,192,2560]{2,1,0:T(8,128)(2,1)S(1)}, u32[]{:S(2)}, u32[]{:S(2)}) %collective-permute-start) | collective-permute-done | bytes 1966112 | tf_op jit(solution)/shard_map/while/body/eval_jaxpr/ppermute | solution.py:14
  735.1 27.0 %collective-permute-done = bf16[2,192,2560]{2,1,0:T(8,128)(2,1)S(1)} collective-permute-done((bf16[2,192,2560]{2,1,0:T(8,128)(2,1)}, bf16[2,192,2560]{2,1,0:T(8,128)(2,1)S(1)}, u32[]{:S(2)}, u32[]{:S(2)}) %collective-permute-start) | collective-permute-done | bytes 1966112 | tf_op jit(solution)/shard_map/while/body/eval_jaxpr/ppermute | solution.py:14
  773.3 27.0 %collective-permute-done = bf16[2,192,2560]{2,1,0:T(8,128)(2,1)S(1)} collective-permute-done((bf16[2,192,2560]{2,1,0:T(8,128)(2,1)}, bf16[2,192,2560]{2,1,0:T(8,128)(2,1)S(1)}, u32[]{:S(2)}, u32[]{:S(2)}) %collective-permute-start) | collective-permute-done | bytes 1966112 | tf_op jit(solution)/shard_map/while/body/eval_jaxpr/ppermute | solution.py:14
  811.6 27.0 %collective-permute-done = bf16[2,192,2560]{2,1,0:T(8,128)(2,1)S(1)} collective-permute-done((bf16[2,192,2560]{2,1,0:T(8,128)(2,1)}, bf16[2,192,2560]{2,1,0:T(8,128)(2,1)S(1)}, u32[]{:S(2)}, u32[]{:S(2)}) %collective-permute-start) | collective-permute-done | bytes 1966112 | tf_op jit(solution)/shard_map/while/body/eval_jaxpr/ppermute | solution.py:14
  849.8 27.0 %collective-permute-done = bf16[2,192,2560]{2,1,0:T(8,128)(2,1)S(1)} collective-permute-done((bf16[2,192,2560]{2,1,0:T(8,128)(2,1)}, bf16[2,192,2560]{2,1,0:T(8,128)(2,1)S(1)}, u32[]{:S(2)}, u32[]{:S(2)}) %collective-permute-start) | collective-permute-done | bytes 1966112 | tf_op jit(solution)/shard_map/while/body/eval_jaxpr/ppermute | solution.py:14
  888.0 27.0 %collective-permute-done = bf16[2,192,2560]{2,1,0:T(8,128)(2,1)S(1)} collective-permute-done((bf16[2,192,2560]{2,1,0:T(8,128)(2,1)}, bf16[2,192,2560]{2,1,0:T(8,128)(2,1)S(1)}, u32[]{:S(2)}, u32[]{:S(2)}) %collective-permute-start) | collective-permute-done | bytes 1966112 | tf_op jit(solution)/shard_map/while/body/eval_jaxpr/ppermute | solution.py:14
  926.2 15.7 %convolution_convert_fusion.1 = bf16[192,5120]{1,0:T(8,128)(2,1)} fusion(bf16[2560,5120]{1,0:T(8,128)(2,1)} %param.15, f32[20,192,128]{2,1,0:T(8,128)} %get-tuple-element.38, f32[20,192]{1,0:T(8,128)S(1)} %get-tuple-element.39), kind=kOutput, calls=%fused_computation.26 | convolution fusion | flops 5035130880 | bytes 30161920 | tf_op jit(solution)/shard_map/dot_general | solution.py:84
  942.0 27.8 %reduce-scatter.2.cloned.1.call-done = bf16[192,2560]{1,0:T(8,128)(2,1)} async-done(((bf16[192,5120]{1,0:T(8,128)(2,1)}), bf16[192,2560]{1,0:T(8,128)(2,1)}) %reduce-scatter.2.cloned.1.call-update) | async-done | bytes 983056 | tf_op jit(solution)/shard_map/reduce_scatter | solution.py:85
  (262 shorter events, 179.0 us)
Async XLA Ops:
  6.5 49.9 %copy-start = (bf16[192,2560]{1,0:T(8,128)(2,1)S(1)}, bf16[192,2560]{1,0:T(8,128)(2,1)}, u32[]{:S(2)}) copy-start(bf16[192,2560]{1,0:T(8,128)(2,1)} %param.9) | copy-start | bytes 2949124
  6.5 13.0 %copy-start.8 = (bf16[448,2560]{1,0:T(8,128)(2,1)S(1)}, bf16[448,2560]{1,0:T(8,128)(2,1)}, u32[]{:S(2)}) copy-start(bf16[448,2560]{1,0:T(8,128)(2,1)} %param.13) | copy-start | bytes 6881284
  8.6 41.7 %all-to-all-start = ((s32[1,16,2]{2,0,1:T(1,128)}), s32[1,16,2]{2,0,1:T(1,128)S(1)}, u32[]{:S(2)}, u32[]{:S(2)}) async-start(s32[1,16,2]{2,0,1:T(1,128)} %copy.51), calls=%async_computation | async-start | bytes 16384 | tf_op jit(solution)/shard_map/all_to_all | solution.py:62
  50.2 7.5 copy-start.6
  50.2 193.4 %all-to-all-start.1 = ((bf16[2,16,2,81920]{3,2,0,1:T(2,128)(2,1)}), bf16[2,16,2,81920]{3,2,0,1:T(2,128)(2,1)}, u32[]{:S(2)}, u32[]{:S(2)}) async-start(bf16[2,16,2,81920]{3,2,0,1:T(2,128)(2,1)} %copy.52), calls=%async_computation.1 | async-start | bytes 20971520 | tf_op jit(solution)/shard_map/all_to_all | solution.py:61
  56.4 4.0 copy-start.7
  56.4 913.4 %reduce-scatter.2.cloned.1.call-start = ((), (), s32[]{:S(2)}) async-start(), calls=%async_computation.3 | async-start | bytes 2949120 | tf_op jit(solution)/shard_map/reduce_scatter | solution.py:85
  289.8 10.1 %copy-start.5 = (f32[20,1024,192]{1,2,0:T(8,128)S(1)}, f32[20,1024,192]{1,2,0:T(8,128)}, u32[]{:S(2)}) copy-start(f32[20,1024,192]{1,2,0:T(8,128)} %get-tuple-element.84) | copy-start | bytes 47185924
  299.9 9.2 copy-start.4
  313.9 66.0 %collective-permute-start = (bf16[2,192,2560]{2,1,0:T(8,128)(2,1)}, bf16[2,192,2560]{2,1,0:T(8,128)(2,1)S(1)}, u32[]{:S(2)}, u32[]{:S(2)}) collective-permute-start(bf16[2,192,2560]{2,1,0:T(8,128)(2,1)} %get-tuple-element.144), channel_id=1, source_target_pairs={{0,2},{2,4},{4,6},{6,8},{8,10},{10,12},{12,14},{14,16},{16,18},{18... | collective-permute-start | bytes 5898248 | tf_op jit(solution)/shard_map/while/body/eval_jaxpr/ppermute | solution.py:14
  384.1 3.2 copy-start.2
  391.1 27.0 %collective-permute-start = (bf16[2,192,2560]{2,1,0:T(8,128)(2,1)}, bf16[2,192,2560]{2,1,0:T(8,128)(2,1)S(1)}, u32[]{:S(2)}, u32[]{:S(2)}) collective-permute-start(bf16[2,192,2560]{2,1,0:T(8,128)(2,1)} %get-tuple-element.144), channel_id=1, source_target_pairs={{0,2},{2,4},{4,6},{6,8},{8,10},{10,12},{12,14},{14,16},{16,18},{18... | collective-permute-start | bytes 5898248 | tf_op jit(solution)/shard_map/while/body/eval_jaxpr/ppermute | solution.py:14
  422.3 3.2 copy-start.2
  429.3 27.0 %collective-permute-start = (bf16[2,192,2560]{2,1,0:T(8,128)(2,1)}, bf16[2,192,2560]{2,1,0:T(8,128)(2,1)S(1)}, u32[]{:S(2)}, u32[]{:S(2)}) collective-permute-start(bf16[2,192,2560]{2,1,0:T(8,128)(2,1)} %get-tuple-element.144), channel_id=1, source_target_pairs={{0,2},{2,4},{4,6},{6,8},{8,10},{10,12},{12,14},{14,16},{16,18},{18... | collective-permute-start | bytes 5898248 | tf_op jit(solution)/shard_map/while/body/eval_jaxpr/ppermute | solution.py:14
  460.5 3.2 copy-start.2
  467.6 27.0 %collective-permute-start = (bf16[2,192,2560]{2,1,0:T(8,128)(2,1)}, bf16[2,192,2560]{2,1,0:T(8,128)(2,1)S(1)}, u32[]{:S(2)}, u32[]{:S(2)}) collective-permute-start(bf16[2,192,2560]{2,1,0:T(8,128)(2,1)} %get-tuple-element.144), channel_id=1, source_target_pairs={{0,2},{2,4},{4,6},{6,8},{8,10},{10,12},{12,14},{14,16},{16,18},{18... | collective-permute-start | bytes 5898248 | tf_op jit(solution)/shard_map/while/body/eval_jaxpr/ppermute | solution.py:14
  498.7 3.2 copy-start.2
  505.8 27.0 %collective-permute-start = (bf16[2,192,2560]{2,1,0:T(8,128)(2,1)}, bf16[2,192,2560]{2,1,0:T(8,128)(2,1)S(1)}, u32[]{:S(2)}, u32[]{:S(2)}) collective-permute-start(bf16[2,192,2560]{2,1,0:T(8,128)(2,1)} %get-tuple-element.144), channel_id=1, source_target_pairs={{0,2},{2,4},{4,6},{6,8},{8,10},{10,12},{12,14},{14,16},{16,18},{18... | collective-permute-start | bytes 5898248 | tf_op jit(solution)/shard_map/while/body/eval_jaxpr/ppermute | solution.py:14
  537.0 3.2 copy-start.2
  544.0 27.0 %collective-permute-start = (bf16[2,192,2560]{2,1,0:T(8,128)(2,1)}, bf16[2,192,2560]{2,1,0:T(8,128)(2,1)S(1)}, u32[]{:S(2)}, u32[]{:S(2)}) collective-permute-start(bf16[2,192,2560]{2,1,0:T(8,128)(2,1)} %get-tuple-element.144), channel_id=1, source_target_pairs={{0,2},{2,4},{4,6},{6,8},{8,10},{10,12},{12,14},{14,16},{16,18},{18... | collective-permute-start | bytes 5898248 | tf_op jit(solution)/shard_map/while/body/eval_jaxpr/ppermute | solution.py:14
  575.2 3.2 copy-start.2
  582.2 27.0 %collective-permute-start = (bf16[2,192,2560]{2,1,0:T(8,128)(2,1)}, bf16[2,192,2560]{2,1,0:T(8,128)(2,1)S(1)}, u32[]{:S(2)}, u32[]{:S(2)}) collective-permute-start(bf16[2,192,2560]{2,1,0:T(8,128)(2,1)} %get-tuple-element.144), channel_id=1, source_target_pairs={{0,2},{2,4},{4,6},{6,8},{8,10},{10,12},{12,14},{14,16},{16,18},{18... | collective-permute-start | bytes 5898248 | tf_op jit(solution)/shard_map/while/body/eval_jaxpr/ppermute | solution.py:14
  613.4 3.2 copy-start.2
  620.5 27.0 %collective-permute-start = (bf16[2,192,2560]{2,1,0:T(8,128)(2,1)}, bf16[2,192,2560]{2,1,0:T(8,128)(2,1)S(1)}, u32[]{:S(2)}, u32[]{:S(2)}) collective-permute-start(bf16[2,192,2560]{2,1,0:T(8,128)(2,1)} %get-tuple-element.144), channel_id=1, source_target_pairs={{0,2},{2,4},{4,6},{6,8},{8,10},{10,12},{12,14},{14,16},{16,18},{18... | collective-permute-start | bytes 5898248 | tf_op jit(solution)/shard_map/while/body/eval_jaxpr/ppermute | solution.py:14
  658.7 27.0 %collective-permute-start = (bf16[2,192,2560]{2,1,0:T(8,128)(2,1)}, bf16[2,192,2560]{2,1,0:T(8,128)(2,1)S(1)}, u32[]{:S(2)}, u32[]{:S(2)}) collective-permute-start(bf16[2,192,2560]{2,1,0:T(8,128)(2,1)} %get-tuple-element.144), channel_id=1, source_target_pairs={{0,2},{2,4},{4,6},{6,8},{8,10},{10,12},{12,14},{14,16},{16,18},{18... | collective-permute-start | bytes 5898248 | tf_op jit(solution)/shard_map/while/body/eval_jaxpr/ppermute | solution.py:14
  696.9 27.0 %collective-permute-start = (bf16[2,192,2560]{2,1,0:T(8,128)(2,1)}, bf16[2,192,2560]{2,1,0:T(8,128)(2,1)S(1)}, u32[]{:S(2)}, u32[]{:S(2)}) collective-permute-start(bf16[2,192,2560]{2,1,0:T(8,128)(2,1)} %get-tuple-element.144), channel_id=1, source_target_pairs={{0,2},{2,4},{4,6},{6,8},{8,10},{10,12},{12,14},{14,16},{16,18},{18... | collective-permute-start | bytes 5898248 | tf_op jit(solution)/shard_map/while/body/eval_jaxpr/ppermute | solution.py:14
  735.1 27.0 %collective-permute-start = (bf16[2,192,2560]{2,1,0:T(8,128)(2,1)}, bf16[2,192,2560]{2,1,0:T(8,128)(2,1)S(1)}, u32[]{:S(2)}, u32[]{:S(2)}) collective-permute-start(bf16[2,192,2560]{2,1,0:T(8,128)(2,1)} %get-tuple-element.144), channel_id=1, source_target_pairs={{0,2},{2,4},{4,6},{6,8},{8,10},{10,12},{12,14},{14,16},{16,18},{18... | collective-permute-start | bytes 5898248 | tf_op jit(solution)/shard_map/while/body/eval_jaxpr/ppermute | solution.py:14
  773.3 27.0 %collective-permute-start = (bf16[2,192,2560]{2,1,0:T(8,128)(2,1)}, bf16[2,192,2560]{2,1,0:T(8,128)(2,1)S(1)}, u32[]{:S(2)}, u32[]{:S(2)}) collective-permute-start(bf16[2,192,2560]{2,1,0:T(8,128)(2,1)} %get-tuple-element.144), channel_id=1, source_target_pairs={{0,2},{2,4},{4,6},{6,8},{8,10},{10,12},{12,14},{14,16},{16,18},{18... | collective-permute-start | bytes 5898248 | tf_op jit(solution)/shard_map/while/body/eval_jaxpr/ppermute | solution.py:14
  811.6 27.0 %collective-permute-start = (bf16[2,192,2560]{2,1,0:T(8,128)(2,1)}, bf16[2,192,2560]{2,1,0:T(8,128)(2,1)S(1)}, u32[]{:S(2)}, u32[]{:S(2)}) collective-permute-start(bf16[2,192,2560]{2,1,0:T(8,128)(2,1)} %get-tuple-element.144), channel_id=1, source_target_pairs={{0,2},{2,4},{4,6},{6,8},{8,10},{10,12},{12,14},{14,16},{16,18},{18... | collective-permute-start | bytes 5898248 | tf_op jit(solution)/shard_map/while/body/eval_jaxpr/ppermute | solution.py:14
  849.8 27.0 %collective-permute-start = (bf16[2,192,2560]{2,1,0:T(8,128)(2,1)}, bf16[2,192,2560]{2,1,0:T(8,128)(2,1)S(1)}, u32[]{:S(2)}, u32[]{:S(2)}) collective-permute-start(bf16[2,192,2560]{2,1,0:T(8,128)(2,1)} %get-tuple-element.144), channel_id=1, source_target_pairs={{0,2},{2,4},{4,6},{6,8},{8,10},{10,12},{12,14},{14,16},{16,18},{18... | collective-permute-start | bytes 5898248 | tf_op jit(solution)/shard_map/while/body/eval_jaxpr/ppermute | solution.py:14
  888.0 27.0 %collective-permute-start = (bf16[2,192,2560]{2,1,0:T(8,128)(2,1)}, bf16[2,192,2560]{2,1,0:T(8,128)(2,1)S(1)}, u32[]{:S(2)}, u32[]{:S(2)}) collective-permute-start(bf16[2,192,2560]{2,1,0:T(8,128)(2,1)} %get-tuple-element.144), channel_id=1, source_target_pairs={{0,2},{2,4},{4,6},{6,8},{8,10},{10,12},{12,14},{14,16},{16,18},{18... | collective-permute-start | bytes 5898248 | tf_op jit(solution)/shard_map/while/body/eval_jaxpr/ppermute | solution.py:14
  926.2 43.6 %copy-start.1 = (bf16[192,2560]{1,0:T(8,128)(2,1)S(1)}, bf16[192,2560]{1,0:T(8,128)(2,1)}, u32[]{:S(2)}) copy-start(bf16[192,2560]{1,0:T(8,128)(2,1)} %param.9) | copy-start | bytes 2949124
  (24 other events, 55.8 us)
Sparse Core Ops, SparseCore 0:
  942.1 27.6 reduce-scatter.1
where the time goes:
time: 978 us; the launch traced here: 977 us
  waiting for transfers between devices  652 us (67%)
  local copies, waits for them, and re-layouts  161 us (16%)
  matrix products  112 us (11%)
  other arithmetic  23 us (2%)
  starting transfers between devices  14.4 us (1%)
  between operations  13.5 us (1%)
    ppermute x15, waiting for transfers between devices, passed_along(): lax.ppermute(value, axis, [(i, (i + by) % length) for i in range(length)])  443 us
    all_to_all x1, waiting for transfers between devices, local(): lax.all_to_all(outgoing, 'seq', split_axis=1, concat_axis=1, tiled=True)  182 us
    dot_general x17, matrix products, attend(): jnp.einsum('qhd,khd->hqk', query_heads, key_heads, preferred_element_type...  49.9 us
    dot_general x17, matrix products, attend(): jnp.einsum('hqk,khd->hqd', weights.astype(jnp.bfloat16), val_heads, prefe...  41.2 us
    while x90, local copies, waits for them, and re-layouts  28.3 us
    reduce_scatter x1, waiting for transfers between devices, local(): lax.psum_scatter(partial_out.astype(jnp.bfloat16), 'head', scatter_dimens...  27.8 us
    slice x16, local copies, waits for them, and re-layouts, attend(): val_heads = key_val[1].reshape(-1, head_count, HDIM)  26.5 us
    squeeze x15, local copies, waits for them, and re-layouts, attend(): val_heads = key_val[1].reshape(-1, head_count, HDIM)  24.9 us
  transfers between devices with their start and end apart: 18, of which 17 were waited for; matrix products, arithmetic and copies ran while one was open for 4% of the time, Pallas kernels for 0%

commit v1 on v0

--- a/solution.py
+++ b/solution.py
@@ -1,12 +1,427 @@
+import functools
 import math
 
 import jax
 import jax.numpy as jnp
 from jax import lax
+from jax.experimental import pallas as pl
+from jax.experimental.pallas import tpu as pltpu
 from jax.sharding import PartitionSpec as P
 
 HDIM = 128
 CAP = 2
+PLANE = 4
+LOG2 = math.log2(math.e) / math.sqrt(HDIM)
+MESH = pl.DeviceIdType.MESH
+F32 = jnp.float32
+BF16 = jnp.bfloat16
+NT = (((1,), (1,)), ((), ()))
+TN = (((0,), (0,)), ((), ()))
+
+
+def kernel(nz, chunks, hc, piece, sel, q_in, k_in, v_in, hk_in, hv_in, out,
+           qx, kb, vb, hkb, hvb, hkw, hvw, ocs, mls, ocr, mlr, r, rml, zlb, zlml, zrb, zrml, fb, bias,
+           q_loc, q_xs, q_xr, kv_loc, kv_xs, kv_xr,
+           qc_s, qc_r, qr_s, qr_r, ql_s, ql_r,
+           oc_s, oc_r, om_s, om_r, zl_s, zl_r, zlm_s, zlm_r, zr_s, zr_r, zrm_s, zrm_r,
+           f_loc, f_s, f_r):
+    s = lax.axis_index("seq")
+    hd = lax.axis_index("head")
+    z, x, c = s // PLANE, (s // 2) % 2, s % 2
+    tok = q_in.shape[0]
+    both = 2 * tok
+    w = hc * HDIM
+    half = chunks * w
+    xp = (z * PLANE + (1 - x) * 2 + c, hd)
+    cp = (z * PLANE + x * 2 + (1 - c), hd)
+    left = (jnp.maximum(s - PLANE, 0), hd)
+    right = (jnp.minimum(s + PLANE, nz * PLANE - 1), hd)
+    has_left, has_right = z > 0, z < nz - 1
+    own = z * 2 + c
+
+    def remote(src, dst, ss, rs, dev):
+        return pltpu.make_async_remote_copy(
+            src_ref=src, dst_ref=dst, send_sem=ss, recv_sem=rs, device_id=dev, device_id_type=MESH)
+
+    def cols(side, k):
+        return pl.ds(pl.multiple_of(side * half + k * w, HDIM), w)
+
+    def q_own(k):
+        return pltpu.make_async_copy(q_in.at[:, cols(x, k)], qx.at[own, k, x], q_loc.at[k])
+
+    def q_cross(k):
+        return remote(q_in.at[:, cols(1 - x, k)], qx.at[own, k, x], q_xs.at[k], q_xr.at[k], xp)
+
+    pairs = ((k_in, kb), (v_in, vb), (hk_in, hkb), (hv_in, hvb))
+
+    def kv_own(k, i):
+        return pltpu.make_async_copy(pairs[i][0].at[:, cols(x, k)], pairs[i][1].at[k, 0], kv_loc.at[i, k])
+
+    def kv_cross(k, i):
+        return remote(pairs[i][0].at[:, cols(1 - x, k)], pairs[i][1].at[k, 1], kv_xs.at[i, k], kv_xr.at[i, k], xp)
+
+    def kv_start(k):
+        for i in range(4):
+            kv_own(k, i).start()
+            kv_cross(k, i).start()
+
+    def q_to(zs, k, which):
+        ss, rs, dev = {"c": (qc_s, qc_r, cp), "r": (qr_s, qr_r, right), "l": (ql_s, ql_r, left)}[which]
+        slot = zs * 2 + c
+        return remote(qx.at[slot, k], qx.at[slot, k], ss.at[zs, k], rs.at[zs, k], dev)
+
+    def q_hop1(k):
+        q_own(k).wait()
+        q_cross(k).wait_recv()
+
+        @pl.when(has_right)
+        def _():
+            q_to(z, k, "r").start()
+
+        @pl.when(has_left)
+        def _():
+            q_to(z, k, "l").start()
+
+        q_to(z, k, "c").start()
+
+    def q_forward(k, d):
+        @pl.when(z - d >= 0)
+        def _():
+            q_to(z - d, k, "r").wait_recv()
+
+            @pl.when(has_right)
+            def _():
+                q_to(z - d, k, "r").start()
+
+            q_to(z - d, k, "c").start()
+
+        @pl.when(z + d < nz)
+        def _():
+            q_to(z + d, k, "l").wait_recv()
+
+            @pl.when(has_left)
+            def _():
+                q_to(z + d, k, "l").start()
+
+            q_to(z + d, k, "c").start()
+
+    def o_core(t, k):
+        return (remote(ocs.at[t, k], ocr.at[t, k], oc_s.at[t, k], oc_r.at[t, k], cp),
+                remote(mls.at[t, k], mlr.at[t, k], om_s.at[t, k], om_r.at[t, k], cp))
+
+    def o_right(t, k):
+        return (remote(r.at[t, k], zlb.at[t, k], zl_s.at[t, k], zl_r.at[t, k], right),
+                remote(rml.at[t, k], zlml.at[t, k], zlm_s.at[t, k], zlm_r.at[t, k], right))
+
+    def o_left(t, k):
+        return (remote(r.at[t, k], zrb.at[t, k], zr_s.at[t, k], zr_r.at[t, k], left),
+                remote(rml.at[t, k], zrml.at[t, k], zrm_s.at[t, k], zrm_r.at[t, k], left))
+
+    def get(o_ref, ml_ref, t, k, h):
+        return (o_ref[t, k, h * HDIM:(h + 1) * HDIM, :].astype(F32),
+                ml_ref[t, k, h * 8:h * 8 + 1, :], ml_ref[t, k, h * 8 + 1:h * 8 + 2, :])
+
+    def put(o_ref, ml_ref, t, k, h, part):
+        o, m, l = part
+        o_ref[t, k, h * HDIM:(h + 1) * HDIM, :] = o.astype(BF16)
+        row = lax.broadcasted_iota(jnp.int32, (8, both), 0)
+        ml_ref[t, k, h * 8:(h + 1) * 8, :] = jnp.where(row == 0, m, l)
+
+    def merge(a, b):
+        m = jnp.maximum(a[1], b[1])
+        fa, fb_ = jnp.exp2((a[1] - m) * LOG2), jnp.exp2((b[1] - m) * LOG2)
+        return a[0] * fa + b[0] * fb_, m, a[2] * fa + b[2] * fb_
+
+    def partial(k, t, cc, h):
+        lanes = slice(h * HDIM, (h + 1) * HDIM)
+        qs = qx[t * 2 + cc, k, :, :, lanes].reshape(both, HDIM)
+        kc = kb[k, :, :, lanes].reshape(both, HDIM)
+        vc = vb[k, :, :, lanes].reshape(both, HDIM)
+        kh, vh = [], []
+        for xx in range(2):
+            b = t * PLANE + xx * 2 + cc
+            for src in range(2):
+                for slot in range(CAP):
+                    n = sel[b, src * 4 + slot]
+                    kh.append(hkw[src, n, :, lanes])
+                    vh.append(hvw[src, n, :, lanes])
+        kh, vh = jnp.concatenate(kh, axis=0), jnp.concatenate(vh, axis=0)
+        s1 = lax.dot_general(kc, qs, NT, preferred_element_type=F32)
+        s2 = lax.dot_general(kh, qs, NT, preferred_element_type=F32) + bias[t * 2 + cc]
+        m = jnp.maximum(jnp.max(s1, axis=0, keepdims=True), jnp.max(s2, axis=0, keepdims=True))
+        p1 = jnp.exp2((s1 - m) * LOG2)
+        p2 = jnp.exp2((s2 - m) * LOG2)
+        l = jnp.sum(p1, axis=0, keepdims=True) + jnp.sum(p2, axis=0, keepdims=True)
+        o = lax.dot_general(vc, p1.astype(BF16), TN, preferred_element_type=F32)
+        o = o + lax.dot_general(vh, p2.astype(BF16), TN, preferred_element_type=F32)
+        return o, m, l
+
+    def rs_step(k, wave):
+        @pl.when((z == wave) & has_right)
+        def _():
+            def one(i, _):
+                t = nz - 1 - i
+
+                @pl.when(t > z)
+                def _():
+                    @pl.when(has_left)
+                    def _():
+                        for cpy in o_right(t, k):
+                            cpy.wait_recv()
+                        for h in range(hc):
+                            put(r, rml, t, k, h, merge(get(r, rml, t, k, h), get(zlb, zlml, t, k, h)))
+                    for cpy in o_right(t, k):
+                        cpy.start()
+                return 0
+            lax.fori_loop(0, nz, one, 0)
+
+        @pl.when((z == nz - 1 - wave) & has_left)
+        def _():
+            def one(t, _):
+                @pl.when(t < z)
+                def _():
+                    @pl.when(has_right)
+                    def _():
+                        for cpy in o_left(t, k):
+                            cpy.wait_recv()
+                        for h in range(hc):
+                            put(r, rml, t, k, h, merge(get(r, rml, t, k, h), get(zrb, zrml, t, k, h)))
+                    for cpy in o_left(t, k):
+                        cpy.start()
+                return 0
+            lax.fori_loop(0, nz, one, 0)
+
+    def final_own(k):
+        return pltpu.make_async_copy(fb.at[k, x], out.at[:, cols(x, k)], f_loc.at[k])
+
+    def final_cross(k):
+        return remote(fb.at[k, 1 - x], out.at[:, cols(x, k)], f_s.at[k], f_r.at[k], xp)
+
+    def final(k):
+        @pl.when(has_left)
+        def _():
+            for cpy in o_right(z, k):
+                cpy.wait_recv()
+            for h in range(hc):
+                put(r, rml, z, k, h, merge(get(r, rml, z, k, h), get(zlb, zlml, z, k, h)))
+
+        @pl.when(has_right)
+        def _():
+            for cpy in o_left(z, k):
+                cpy.wait_recv()
+            for h in range(hc):
+                put(r, rml, z, k, h, merge(get(r, rml, z, k, h), get(zrb, zrml, z, k, h)))
+
+        for h in range(hc):
+            o, _, l = get(r, rml, z, k, h)
+            done = jnp.transpose(o / l).astype(BF16)
+            fb[k, :, :, h * HDIM:(h + 1) * HDIM] = done.reshape(2, tok, HDIM)
+        final_own(k).start()
+        final_cross(k).start()
+
+    barrier = pltpu.get_barrier_semaphore()
+    for dev in (xp, cp):
+        pl.semaphore_signal(barrier, inc=1, device_id=dev, device_id_type=MESH)
+
+    @pl.when(has_left)
+    def _():
+        pl.semaphore_signal(barrier, inc=1, device_id=left, device_id_type=MESH)
+
+    @pl.when(has_right)
+    def _():
+        pl.semaphore_signal(barrier, inc=1, device_id=right, device_id_type=MESH)
+
+    pl.semaphore_wait(barrier, 2 + has_left.astype(jnp.int32) + has_right.astype(jnp.int32))
+
+    for k in range(chunks):
+        q_cross(k).start()
+        q_own(k).start()
+    for k in range(min(2, chunks)):
+        kv_start(k)
+
+    block_of = lax.broadcasted_iota(jnp.int32, (piece, both), 1) // tok
+
+    def fill(i, _):
+        t, cc = i // 2, i % 2
+        for xx in range(2):
+            b = t * PLANE + xx * 2 + cc
+            for src in range(2):
+                for slot in range(CAP):
+                    n = (xx * 2 + src) * CAP + slot
+                    live = (sel[b, src * 4 + CAP + slot].astype(F32) - 1.0) * 1e30
+                    bias[i, n * piece:(n + 1) * piece, :] = jnp.where(block_of == xx, live, -1e30)
+        return 0
+
+    lax.fori_loop(0, nz * 2, fill, 0)
+
+    for k in range(min(2, chunks)):
+        q_hop1(k)
+    for d in range(1, nz):
+        q_forward(0, d)
+
+    def slot_body(j, _):
+        k, second = j // 2, j % 2
+
+        @pl.when((k < chunks) & (second == 0))
+        def _():
+            for i in range(4):
+                kv_own(k, i).wait()
+                kv_cross(k, i).wait_recv()
+
+            @pl.when(k + 2 < chunks)
+            def _():
+                kv_start(k + 2)
+                q_hop1(k + 2)
+            hkw[...] = hkb[k].reshape(hkw.shape)
+            hvw[...] = hvb[k].reshape(hvw.shape)
+
+            def got(zs, _):
+                q_to(zs, k, "c").wait_recv()
+                return 0
+            lax.fori_loop(0, nz, got, 0)
+
+        @pl.when((k + 1 < chunks) & (second == 0))
+        def _():
+            q_forward(k + 1, 1)
+
+        @pl.when((k + 1 < chunks) & (second == 1))
+        def _():
+            for d in range(2, nz):
+                q_forward(k + 1, d)
+
+        @pl.when(k < chunks)
+        def _():
+            cc = jnp.where(second == 0, 1 - c, c)
+
+            def target(t, _):
+                parts = [partial(k, t, cc, h) for h in range(hc)]
+
+                @pl.when(second == 0)
+                def _():
+                    for h in range(hc):
+                        put(ocs, mls, t, k, h, parts[h])
+                    for cpy in o_core(t, k):
+                        cpy.start()
+
+                @pl.when(second == 1)
+                def _():
+                    for cpy in o_core(t, k):
+                        cpy.wait_recv()
+                    for h in range(hc):
+                        put(r, rml, t, k, h, merge(parts[h], get(ocr, mlr, t, k, h)))
+                return 0
+            lax.fori_loop(0, nz, target, 0)
+
+        def waves(i, _):
+            wave = nz - 1 - i
+            age = j - 1 - wave
+            kk = age // 2
+
+            @pl.when((age >= 0) & (age % 2 == 0) & (kk < chunks))
+            def _():
+                rs_step(kk, wave)
+
+                @pl.when(wave == nz - 1)
+                def _():
+                    final(kk)
+            return 0
+        lax.fori_loop(0, nz, waves, 0)
+        return 0
+
+    lax.fori_loop(0, 2 * chunks + nz, slot_body, 0)
+
+    def drain(k, _):
+        q_cross(k).wait_send()
+        for i in range(4):
+            kv_cross(k, i).wait_send()
+        final_own(k).wait()
+        final_cross(k).wait()
+
+        def each(t, _):
+            q_to(t, k, "c").wait_send()
+            for cpy in o_core(t, k):
+                cpy.wait_send()
+
+            @pl.when(has_right & (t <= z))
+            def _():
+                q_to(t, k, "r").wait_send()
+
+            @pl.when(has_left & (t >= z))
+            def _():
+                q_to(t, k, "l").wait_send()
+
+            @pl.when(t > z)
+            def _():
+                for cpy in o_right(t, k):
+                    cpy.wait_send()
+
+            @pl.when(t < z)
+            def _():
+                for cpy in o_left(t, k):
+                    cpy.wait_send()
+            return 0
+        lax.fori_loop(0, nz, each, 0)
+        return 0
+
+    lax.fori_loop(0, chunks, drain, 0)
+
+
+def reader_table(piece_readers, readers):
+    hits = jnp.any(piece_readers[:, :, None] == jnp.arange(readers, dtype=jnp.int32)[None, None, :], axis=1)
+    hits = hits.astype(jnp.int32)
+    rank = jnp.cumsum(hits, axis=0) - hits
+    index = jnp.arange(piece_readers.shape[0], dtype=jnp.int32)[:, None]
+    where = [jnp.sum(jnp.where((hits > 0) & (rank == n), index, 0), axis=0) for n in range(CAP)]
+    count = jnp.sum(hits, axis=0)
+    return jnp.stack(where + [(count > n).astype(jnp.int32) for n in range(CAP)], axis=1)
+
+
+def fused_attention(queries, cur_keys, cur_values, hist_keys, hist_values, piece_readers):
+    tok, width = queries.shape
+    hist = hist_keys.shape[0]
+    readers = lax.axis_size("seq")
+    nz = readers // PLANE
+    half_heads = width // HDIM // 2
+    hc = 2 if half_heads % 2 == 0 else 1
+    chunks = half_heads // hc
+    w = hc * HDIM
+    both = 2 * tok
+    piece = hist // piece_readers.shape[0]
+    table = reader_table(piece_readers, readers)
+    other = lax.ppermute(table, "seq", [(i, i ^ 2) for i in range(readers)])
+    sel = jnp.concatenate([table, other], axis=1)
+    vm = pltpu.VMEM
+    sem = pltpu.SemaphoreType.DMA
+    o_buf = vm((nz, chunks, w, both), BF16)
+    ml_buf = vm((nz, chunks, hc * 8, both), F32)
+    scratch = [
+        vm((nz * 2, chunks, 2, tok, w), BF16),
+        vm((chunks, 2, tok, w), BF16), vm((chunks, 2, tok, w), BF16),
+        vm((chunks, 2, hist, w), BF16), vm((chunks, 2, hist, w), BF16),
+        vm((2, hist // piece, piece, w), BF16), vm((2, hist // piece, piece, w), BF16),
+        o_buf, ml_buf, o_buf, ml_buf, o_buf, ml_buf, o_buf, ml_buf, o_buf, ml_buf,
+        vm((chunks, 2, tok, w), BF16),
+        vm((nz * 2, 4 * CAP * piece, both), F32),
+    ]
+    scratch += [sem((chunks,))] * 3 + [sem((4, chunks))] * 3 + [sem((nz, chunks))] * 18 + [sem((chunks,))] * 3
+    any_spec = pl.BlockSpec(memory_space=pl.ANY)
+    flops = 4 * readers * tok * (2 * tok + 4 * CAP * piece) * width // 2
+    return pl.pallas_call(
+        functools.partial(kernel, nz, chunks, hc, piece),
+        out_shape=jax.ShapeDtypeStruct((tok, width), BF16),
+        in_specs=[pl.BlockSpec(memory_space=pltpu.SMEM)] + [any_spec] * 5,
+        out_specs=any_spec,
+        scratch_shapes=scratch,
+        compiler_params=pltpu.CompilerParams(
+            collective_id=0, has_side_effects=True, vmem_limit_bytes=60 * 1024 * 1024),
+        cost_estimate=pl.CostEstimate(flops=flops, bytes_accessed=12 * tok * width, transcendentals=flops // 512),
+    )(sel, queries, cur_keys, cur_values, hist_keys, hist_values)
+
+
+def local_fused(queries, cur_keys, cur_values, hist_keys, hist_values, piece_readers, out_weight):
+    attended = fused_attention(queries, cur_keys, cur_values, hist_keys, hist_values, piece_readers)
+    partial_out = jnp.dot(attended, out_weight, preferred_element_type=F32)
+    return lax.psum_scatter(partial_out.astype(BF16), "head", scatter_dimension=1, tiled=True)
 
 
 def passed_along(value, axis, by):
@@ -97,6 +512,13 @@
         P("seq", None),
         P("head", None),
     )
-    return jax.shard_map(
-        local, mesh=mesh, in_specs=placed, out_specs=P("seq", "head"), check_vma=False
-    )
+
+    def run(*args):
+        heads = args[0].shape[1] // mesh.shape["head"] // HDIM
+        whole_planes = mesh.shape["seq"] % PLANE == 0 and heads % 2 == 0
+        return jax.shard_map(
+            local_fused if whole_planes else local,
+            mesh=mesh, in_specs=placed, out_specs=P("seq", "head"), check_vma=False,
+        )(*args)
+
+    return run

time: 978 us -> 208 us (0.21)
  waiting for transfers between devices: 652 us -> 31.9 us
  local copies, waits for them, and re-layouts: 161 us -> 1.09 us
  Pallas kernels: 0 us -> 146 us
  matrix products: 112 us -> 12.5 us
  other arithmetic: 23 us -> 0.84 us
  starting transfers between devices: 14.4 us -> 2.94 us
    ppermute x15 -> x1, waiting for transfers between devices: 443 us -> 1.29 us  [fused_attention(): other = lax.ppermute(table, 'seq', [(i, i ^ 2) for i in range(readers)])]
    all_to_all x2 -> x0, waiting for transfers between devices: 182 us -> none  [the longest x1 182 us: local(): lax.all_to_all(outgoing, 'seq', split_axis=1, concat_axis=1, tiled=True)]
    pallas_call x0 -> x1, Pallas kernels: none -> 146 us  [fused_attention(): pl.pallas_call(functools.partial(kernel, nz, chunks, hc, piece), out_shap...]
    dot_general x36 -> x1, matrix products: 112 us -> 12.5 us  [local_fused(): partial_out = jnp.dot(attended, out_weight, preferred_element_type=F32)]
    squeeze x30 -> x0, local copies, waits for them, and re-layouts: 46.7 us -> none  [the longest x15 24.9 us: attend(): val_heads = key_val[1].reshape(-1, head_count, HDIM)]
    another operation x4 -> x3, local copies, waits for them, and re-layouts: 32.1 us -> 0.25 us  [reader_table(): jnp.stack(where + [(count > n).astype(jnp.int32) for n in range(CAP)], ax...]
    while x90 -> x0, local copies, waits for them, and re-layouts: 28.3 us -> none
    slice x16 -> x0, local copies, waits for them, and re-layouts: 26.5 us -> none  [attend(): val_heads = key_val[1].reshape(-1, head_count, HDIM)]
  transfers between devices with their start and end apart: 18 -> 2, of which waited for: 17 -> 2; matrix products, arithmetic and copies ran while one was open for 4% -> 0% of each run, Pallas kernels for 0% -> 0%
where the time goes in v1:
time: 208 us
  Pallas kernels  146 us (70%)
  waiting for transfers between devices  31.9 us (15%)
  between operations  13.4 us (6%)
  matrix products  12.5 us (6%)
  starting transfers between devices  2.94 us (1%)
    pallas_call x1, Pallas kernels, fused_attention(): pl.pallas_call(functools.partial(kernel, nz, chunks, hc, piece), out_shap...  146 us
    reduce_scatter x1, waiting for transfers between devices, local_fused(): lax.psum_scatter(partial_out.astype(BF16), 'head', scatter_dimension=1, t...  30.6 us
    dot_general x1, matrix products, local_fused(): partial_out = jnp.dot(attended, out_weight, preferred_element_type=F32)  12.5 us
  transfers between devices with their start and end apart: 2, of which 2 were waited for; matrix products, arithmetic and copies ran while one was open for 0% of the time, Pallas kernels for 0%

profile of v1, /device:TPU:0, one launch (start us, length us, event | category | flops | bytes accessed | tf_op | source)
XLA Modules:
  0.0 208.3 jit_solution(9624389106678078971)
XLA Ops:
  6.5 0.0 reduce-scatter.2.cloned.1.call-start
  6.5 0.8 fusion
  7.4 0.1 copy.23
  7.5 2.9 %collective-permute-start = (s32[16,4]{1,0:T(8,128)S(1)}, s32[16,4]{1,0:T(8,128)S(1)}, u32[]{:S(2)}, u32[]{:S(2)}) collective-permute-start(s32[16,4]{1,0:T(8,128)S(1)} %copy.23), channel_id=1, source_target_pairs={{0,4},{2,6},{4,0},{6,2},{8,12},{10,14},{12,8},{14,10},{16,20},{18,... | collective-permute-start | bytes 776 | tf_op jit(solution)/shard_map/ppermute | solution.py:391
  10.4 0.1 copy.24
  10.5 0.1 copy.25
  10.6 0.1 copy.26
  10.7 0.1 copy.27
  10.7 1.3 collective-permute-done
  12.0 0.7 concatenate.4.sel
  12.7 145.6 %shard_map.73 = bf16[192,2560]{1,0:T(8,128)(2,1)} custom-call(s32[16,8]{1,0:T(8,128)} %concatenate.4.sel, bf16[192,2560]{1,0:T(8,128)(2,1)} %q_in.1, bf16[192,2560]{1,0:T(8,128)(2,1)} %k_in.1, bf16[192,2560]{1,0:T(8,128)(2,1)} %v_in.1, bf16[448,2560]{1,0:T(8,128)(2,1)} %hk_in.1, bf16[448,2560]{1,0:T(8,128)(2,1)} %hv_in.1), custom_call_target="tpu_custom_call" | custom-call | flops 10066329600 | bytes 5898240 | tf_op jit(solution)/shard_map/pallas_call | solution.py:409
  158.4 12.5 %convolution_convert_fusion = bf16[192,5120]{1,0:T(8,128)(2,1)} fusion(bf16[192,2560]{1,0:T(8,128)(2,1)} %shard_map.73, bf16[2560,5120]{1,0:T(8,128)(2,1)} %param.13), kind=kOutput, calls=%fused_computation | convolution fusion | flops 5034147840 | bytes 29163520 | tf_op jit(solution)/shard_map/dot_general | solution.py:423
  170.8 0.0 reduce-scatter.2.cloned.1.call-update
  170.8 30.6 %reduce-scatter.2.cloned.1.call-done = bf16[192,2560]{1,0:T(8,128)(2,1)} async-done(((bf16[192,5120]{1,0:T(8,128)(2,1)}), bf16[192,2560]{1,0:T(8,128)(2,1)}) %reduce-scatter.2.cloned.1.call-update) | async-done | bytes 983056 | tf_op jit(solution)/shard_map/reduce_scatter | solution.py:424
  (5 shorter events, 0.1 us)
Async XLA Ops:
  6.5 194.9 %reduce-scatter.2.cloned.1.call-start = ((), (), s32[]{:S(2)}) async-start(), calls=%async_computation.1 | async-start | bytes 2949120 | tf_op jit(solution)/shard_map/reduce_scatter | solution.py:424
  7.5 4.6 %collective-permute-start = (s32[16,4]{1,0:T(8,128)S(1)}, s32[16,4]{1,0:T(8,128)S(1)}, u32[]{:S(2)}, u32[]{:S(2)}) collective-permute-start(s32[16,4]{1,0:T(8,128)S(1)} %copy.23), channel_id=1, source_target_pairs={{0,4},{2,6},{4,0},{6,2},{8,12},{10,14},{12,8},{14,10},{16,20},{18,... | collective-permute-start | bytes 776 | tf_op jit(solution)/shard_map/ppermute | solution.py:391
Sparse Core Ops, SparseCore 0:
  171.0 30.4 reduce-scatter.1

commit v2 on v1

--- a/solution.py
+++ b/solution.py
@@ -19,12 +19,13 @@
 TN = (((0,), (0,)), ((), ()))
 
 
-def kernel(nz, chunks, hc, piece, sel, q_in, k_in, v_in, hk_in, hv_in, out,
-           qx, kb, vb, hkb, hvb, hkw, hvw, ocs, mls, ocr, mlr, r, rml, zlb, zlml, zrb, zrml, fb, bias,
+def kernel(nz, chunks, hc, piece, sel, q_in, k_in, v_in, hk_in, hv_in, w_in, out,
+           qx, kb, vb, hkb, hvb, hkw, hvw, ocs, mls, ocr, mlr, r, rml, zlb, zlml, zrb, zrml, fs, att, bias,
+           wbuf, acc, ysend, yrecv,
            q_loc, q_xs, q_xr, kv_loc, kv_xs, kv_xr,
            qc_s, qc_r, qr_s, qr_r, ql_s, ql_r,
            oc_s, oc_r, om_s, om_r, zl_s, zl_r, zlm_s, zlm_r, zr_s, zr_r, zrm_s, zrm_r,
-           f_loc, f_s, f_r):
+           w_sem, f_s, f_r, y_s, y_r):
     s = lax.axis_index("seq")
     hd = lax.axis_index("head")
     z, x, c = s // PLANE, (s // 2) % 2, s % 2
@@ -36,6 +37,8 @@
     cp = (z * PLANE + x * 2 + (1 - c), hd)
     left = (jnp.maximum(s - PLANE, 0), hd)
     right = (jnp.minimum(s + PLANE, nz * PLANE - 1), hd)
+    yp = (s, 1 - hd)
+    tiles, _, tile = ysend.shape
     has_left, has_right = z > 0, z < nz - 1
     own = z * 2 + c
 
@@ -191,11 +194,39 @@
                 return 0
             lax.fori_loop(0, nz, one, 0)
 
-    def final_own(k):
-        return pltpu.make_async_copy(fb.at[k, x], out.at[:, cols(x, k)], f_loc.at[k])
-
     def final_cross(k):
-        return remote(fb.at[k, 1 - x], out.at[:, cols(x, k)], f_s.at[k], f_r.at[k], xp)
+        return remote(fs.at[k], att.at[x, k], f_s.at[k], f_r.at[k], xp)
+
+    def w_fetch(k, side):
+        rows = pl.ds(pl.multiple_of(side * half + k * w, HDIM), w)
+        return pltpu.make_async_copy(w_in.at[rows], wbuf.at[k % 2, side], w_sem.at[side, k])
+
+    def y_cross(i):
+        return remote(ysend.at[i], yrecv.at[i], y_s.at[i], y_r.at[i], yp)
+
+    def project(k):
+        final_cross(k).wait_recv()
+        for side in range(2):
+            w_fetch(k, side).wait()
+        a = jnp.concatenate([att[0, k], att[1, k]], axis=1)
+
+        def one(i, _):
+            lanes = pl.ds(pl.multiple_of(((1 - hd) * tiles + i) % (2 * tiles) * tile, tile), tile)
+            b = wbuf[k % 2, :, :, lanes].reshape(2 * w, tile)
+            value = acc[:, lanes] + jnp.dot(a, b, preferred_element_type=F32)
+            acc[:, lanes] = value
+
+            @pl.when((k == chunks - 1) & (i < tiles))
+            def _():
+                ysend[i] = value.astype(BF16)
+                y_cross(i).start()
+            return 0
+        lax.fori_loop(0, 2 * tiles, one, 0)
+
+        @pl.when(k + 2 < chunks)
+        def _():
+            for side in range(2):
+                w_fetch(k + 2, side).start()
 
     def final(k):
         @pl.when(has_left)
@@ -215,12 +246,14 @@
         for h in range(hc):
             o, _, l = get(r, rml, z, k, h)
             done = jnp.transpose(o / l).astype(BF16)
-            fb[k, :, :, h * HDIM:(h + 1) * HDIM] = done.reshape(2, tok, HDIM)
-        final_own(k).start()
+            lanes = slice(h * HDIM, (h + 1) * HDIM)
+            mine, theirs = done[:tok], done[tok:]
+            att[x, k, :, lanes] = jnp.where(x == 0, mine, theirs)
+            fs[k, :, lanes] = jnp.where(x == 0, theirs, mine)
         final_cross(k).start()
 
     barrier = pltpu.get_barrier_semaphore()
-    for dev in (xp, cp):
+    for dev in (xp, cp, yp):
         pl.semaphore_signal(barrier, inc=1, device_id=dev, device_id_type=MESH)
 
     @pl.when(has_left)
@@ -231,13 +264,17 @@
     def _():
         pl.semaphore_signal(barrier, inc=1, device_id=right, device_id_type=MESH)
 
-    pl.semaphore_wait(barrier, 2 + has_left.astype(jnp.int32) + has_right.astype(jnp.int32))
+    pl.semaphore_wait(barrier, 3 + has_left.astype(jnp.int32) + has_right.astype(jnp.int32))
 
     for k in range(chunks):
         q_cross(k).start()
         q_own(k).start()
     for k in range(min(2, chunks)):
         kv_start(k)
+    for k in range(min(2, chunks)):
+        for side in range(2):
+            w_fetch(k, side).start()
+    acc[...] = jnp.zeros_like(acc)
 
     block_of = lax.broadcasted_iota(jnp.int32, (piece, both), 1) // tok
 
@@ -254,10 +291,11 @@
 
     lax.fori_loop(0, nz * 2, fill, 0)
 
-    for k in range(min(2, chunks)):
+    for k in range(min(nz + 1, chunks)):
         q_hop1(k)
-    for d in range(1, nz):
-        q_forward(0, d)
+    for k in range(min(nz - 1, chunks)):
+        for d in range(1, nz - k):
+            q_forward(k, d)
 
     def slot_body(j, _):
         k, second = j // 2, j % 2
@@ -271,7 +309,15 @@
             @pl.when(k + 2 < chunks)
             def _():
                 kv_start(k + 2)
-                q_hop1(k + 2)
+
+            @pl.when(k + nz + 1 < chunks)
+            def _():
+                q_hop1(k + nz + 1)
+
+            for d in range(1, nz):
+                @pl.when(k + nz - d < chunks)
+                def _():
+                    q_forward(k + nz - d, d)
             hkw[...] = hkb[k].reshape(hkw.shape)
             hvw[...] = hvb[k].reshape(hvw.shape)
 
@@ -280,41 +326,37 @@
                 return 0
             lax.fori_loop(0, nz, got, 0)
 
-        @pl.when((k + 1 < chunks) & (second == 0))
-        def _():
-            q_forward(k + 1, 1)
-
-        @pl.when((k + 1 < chunks) & (second == 1))
-        def _():
-            for d in range(2, nz):
-                q_forward(k + 1, d)
-
         @pl.when(k < chunks)
         def _():
             cc = jnp.where(second == 0, 1 - c, c)
 
-            def target(t, _):
-                parts = [partial(k, t, cc, h) for h in range(hc)]
+            step = 2 if nz % 2 == 0 else 1
+
+            def target(i, _):
+                jobs = [(i * step + u, h) for u in range(step) for h in range(hc)]
+                parts = [partial(k, t, cc, h) for t, h in jobs]
 
                 @pl.when(second == 0)
                 def _():
-                    for h in range(hc):
-                        put(ocs, mls, t, k, h, parts[h])
-                    for cpy in o_core(t, k):
-                        cpy.start()
+                    for (t, h), part in zip(jobs, parts):
+                        put(ocs, mls, t, k, h, part)
+                    for u in range(step):
+                        for cpy in o_core(i * step + u, k):
+                            cpy.start()
 
                 @pl.when(second == 1)
                 def _():
-                    for cpy in o_core(t, k):
-                        cpy.wait_recv()
-                    for h in range(hc):
-                        put(r, rml, t, k, h, merge(parts[h], get(ocr, mlr, t, k, h)))
+                    for u in range(step):
+                        for cpy in o_core(i * step + u, k):
+                            cpy.wait_recv()
+                    for (t, h), part in zip(jobs, parts):
+                        put(r, rml, t, k, h, merge(part, get(ocr, mlr, t, k, h)))
                 return 0
-            lax.fori_loop(0, nz, target, 0)
+            lax.fori_loop(0, nz // step, target, 0)
 
         def waves(i, _):
             wave = nz - 1 - i
-            age = j - 1 - wave
+            age = j - 1 - 2 * wave
             kk = age // 2
 
             @pl.when((age >= 0) & (age % 2 == 0) & (kk < chunks))
@@ -326,16 +368,29 @@
                     final(kk)
             return 0
         lax.fori_loop(0, nz, waves, 0)
+        ready = j - 2 * nz
+
+        @pl.when((ready >= 0) & (ready % 2 == 0))
+        def _():
+            project(ready // 2)
         return 0
 
-    lax.fori_loop(0, 2 * chunks + nz, slot_body, 0)
+    lax.fori_loop(0, 2 * chunks + 2 * nz - 1, slot_body, 0)
+
+    def finish(i, _):
+        y_cross(i).wait_recv()
+        lanes = pl.ds(pl.multiple_of((hd * tiles + i) * tile, tile), tile)
+        out[:, pl.ds(pl.multiple_of(i * tile, tile), tile)] = (acc[:, lanes] + yrecv[i].astype(F32)).astype(BF16)
+        y_cross(i).wait_send()
+        return 0
+
+    lax.fori_loop(0, tiles, finish, 0)
 
     def drain(k, _):
         q_cross(k).wait_send()
         for i in range(4):
             kv_cross(k, i).wait_send()
-        final_own(k).wait()
-        final_cross(k).wait()
+        final_cross(k).wait_send()
 
         def each(t, _):
             q_to(t, k, "c").wait_send()
@@ -376,13 +431,16 @@
     return jnp.stack(where + [(count > n).astype(jnp.int32) for n in range(CAP)], axis=1)
 
 
-def fused_attention(queries, cur_keys, cur_values, hist_keys, hist_values, piece_readers):
+def local_fused(queries, cur_keys, cur_values, hist_keys, hist_values, piece_readers, out_weight):
     tok, width = queries.shape
     hist = hist_keys.shape[0]
     readers = lax.axis_size("seq")
     nz = readers // PLANE
     half_heads = width // HDIM // 2
-    hc = 2 if half_heads % 2 == 0 else 1
+    hc = 1
+    out_width = out_weight.shape[1]
+    tile = 512 if out_width % 1024 == 0 else HDIM
+    tiles = out_width // 2 // tile
     chunks = half_heads // hc
     w = hc * HDIM
     both = 2 * tok
@@ -400,28 +458,25 @@
         vm((chunks, 2, hist, w), BF16), vm((chunks, 2, hist, w), BF16),
         vm((2, hist // piece, piece, w), BF16), vm((2, hist // piece, piece, w), BF16),
         o_buf, ml_buf, o_buf, ml_buf, o_buf, ml_buf, o_buf, ml_buf, o_buf, ml_buf,
-        vm((chunks, 2, tok, w), BF16),
+        vm((chunks, tok, w), BF16), vm((2, chunks, tok, w), BF16),
         vm((nz * 2, 4 * CAP * piece, both), F32),
+        vm((2, 2, w, out_width), BF16), vm((tok, out_width), F32),
+        vm((tiles, tok, tile), BF16), vm((tiles, tok, tile), BF16),
     ]
-    scratch += [sem((chunks,))] * 3 + [sem((4, chunks))] * 3 + [sem((nz, chunks))] * 18 + [sem((chunks,))] * 3
+    scratch += [sem((chunks,))] * 3 + [sem((4, chunks))] * 3 + [sem((nz, chunks))] * 18
+    scratch += [sem((2, chunks))] + [sem((chunks,))] * 2 + [sem((tiles,))] * 2
     any_spec = pl.BlockSpec(memory_space=pl.ANY)
     flops = 4 * readers * tok * (2 * tok + 4 * CAP * piece) * width // 2
     return pl.pallas_call(
         functools.partial(kernel, nz, chunks, hc, piece),
-        out_shape=jax.ShapeDtypeStruct((tok, width), BF16),
-        in_specs=[pl.BlockSpec(memory_space=pltpu.SMEM)] + [any_spec] * 5,
-        out_specs=any_spec,
+        out_shape=jax.ShapeDtypeStruct((tok, out_width // 2), BF16),
+        in_specs=[pl.BlockSpec(memory_space=pltpu.SMEM)] + [any_spec] * 6,
+        out_specs=pl.BlockSpec(memory_space=pltpu.VMEM),
         scratch_shapes=scratch,
         compiler_params=pltpu.CompilerParams(
-            collective_id=0, has_side_effects=True, vmem_limit_bytes=60 * 1024 * 1024),
+            collective_id=0, has_side_effects=True, vmem_limit_bytes=62 * 1024 * 1024),
         cost_estimate=pl.CostEstimate(flops=flops, bytes_accessed=12 * tok * width, transcendentals=flops // 512),
-    )(sel, queries, cur_keys, cur_values, hist_keys, hist_values)
-
-
-def local_fused(queries, cur_keys, cur_values, hist_keys, hist_values, piece_readers, out_weight):
-    attended = fused_attention(queries, cur_keys, cur_values, hist_keys, hist_values, piece_readers)
-    partial_out = jnp.dot(attended, out_weight, preferred_element_type=F32)
-    return lax.psum_scatter(partial_out.astype(BF16), "head", scatter_dimension=1, tiled=True)
+    )(sel, queries, cur_keys, cur_values, hist_keys, hist_values, out_weight)
 
 
 def passed_along(value, axis, by):
@@ -515,7 +570,7 @@
 
     def run(*args):
         heads = args[0].shape[1] // mesh.shape["head"] // HDIM
-        whole_planes = mesh.shape["seq"] % PLANE == 0 and heads % 2 == 0
+        whole_planes = mesh.shape["seq"] % PLANE == 0 and heads % 2 == 0 and mesh.shape["head"] == 2
         return jax.shard_map(
             local_fused if whole_planes else local,
             mesh=mesh, in_specs=placed, out_specs=P("seq", "head"), check_vma=False,

time: 208 us -> 172 us (0.83)
  waiting for transfers between devices: 31.9 us -> 1.3 us
  Pallas kernels: 146 us -> 163 us
  between operations: 13.4 us -> 0.02 us
  matrix products: 12.5 us -> 0 us
  local copies, waits for them, and re-layouts: 1.09 us -> 3.3 us
    reduce_scatter x1 -> x0, waiting for transfers between devices: 30.6 us -> none  [local_fused(): lax.psum_scatter(partial_out.astype(BF16), 'head', scatter_dimension=1, t...]
    pallas_call x1, Pallas kernels: 146 us -> 163 us  [local_fused(): pl.pallas_call(functools.partial(kernel, nz, chunks, hc, piece), out_shap...]
    dot_general x1 -> x0, matrix products: 12.5 us -> none  [local_fused(): partial_out = jnp.dot(attended, out_weight, preferred_element_type=F32)]
    unnamed x0 -> x1, local copies, waits for them, and re-layouts: none -> 2.21 us
  transfers between devices with their start and end apart: 2 -> 1, of which waited for: 2 -> 1; matrix products, arithmetic and copies ran while one was open for 0% -> 0% of each run, Pallas kernels for 0% -> 0%
where the time goes in v2:
time: 172 us
  Pallas kernels  163 us (95%)
  local copies, waits for them, and re-layouts  3.3 us (2%)
  starting transfers between devices  2.94 us (2%)
    pallas_call x1, Pallas kernels, local_fused(): pl.pallas_call(functools.partial(kernel, nz, chunks, hc, piece), out_shap...  163 us
  transfers between devices with their start and end apart: 1, of which 1 were waited for; matrix products, arithmetic and copies ran while one was open for 0% of the time, Pallas kernels for 0%

profile of v2, /device:TPU:0, one launch (start us, length us, event | category | flops | bytes accessed | tf_op | source)
XLA Modules:
  0.0 171.8 jit_solution(10800043078365100317)
XLA Ops:
  0.0 0.8 fusion
  0.8 0.1 copy.23
  0.9 2.9 %collective-permute-start = (s32[16,4]{1,0:T(8,128)S(1)}, s32[16,4]{1,0:T(8,128)S(1)}, u32[]{:S(2)}, u32[]{:S(2)}) collective-permute-start(s32[16,4]{1,0:T(8,128)S(1)} %copy.23), channel_id=1, source_target_pairs={{0,4},{2,6},{4,0},{6,2},{8,12},{10,14},{12,8},{14,10},{16,20},{18,... | collective-permute-start | bytes 776 | tf_op jit(solution)/shard_map/ppermute | solution.py:449
  3.9 0.1 copy.24
  4.0 0.1 copy.25
  4.0 0.1 copy.26
  4.1 0.1 copy.27
  4.2 1.3 collective-permute-done
  5.5 0.7 concatenate.4.sel
  6.2 163.4 %shard_map.73 = bf16[192,2560]{1,0:T(8,128)(2,1)} custom-call(s32[16,8]{1,0:T(8,128)} %concatenate.4.sel, bf16[192,2560]{1,0:T(8,128)(2,1)} %q_in.1, bf16[192,2560]{1,0:T(8,128)(2,1)} %k_in.1, bf16[192,2560]{1,0:T(8,128)(2,1)} %v_in.1, bf16[448,2560]{1,0:T(8,128)(2,1)} %hk_in.1, bf16[448,2560]{1,0:T(8,128)(2,1)} %hv_in.1, bf16[2560,5120]{1,0:T(8,128)(2,1)} %w_in.1), custom_call_target="tpu_custom_call" | custom-call | flops 10066329600 | bytes 5898240 | tf_op jit(solution)/shard_map/pallas_call | solution.py:470
  169.5 2.2 %copy.29 = bf16[192,2560]{1,0:T(8,128)(2,1)} copy(bf16[192,2560]{1,0:T(8,128)(2,1)} %shard_map.73) | data formatting | bytes 1966080
  (5 shorter events, 0.1 us)
Async XLA Ops:
  0.9 4.6 %collective-permute-start = (s32[16,4]{1,0:T(8,128)S(1)}, s32[16,4]{1,0:T(8,128)S(1)}, u32[]{:S(2)}, u32[]{:S(2)}) collective-permute-start(s32[16,4]{1,0:T(8,128)S(1)} %copy.23), channel_id=1, source_target_pairs={{0,4},{2,6},{4,0},{6,2},{8,12},{10,14},{12,8},{14,10},{16,20},{18,... | collective-permute-start | bytes 776 | tf_op jit(solution)/shard_map/ppermute | solution.py:449

commit v3 on v2

--- a/solution.py
+++ b/solution.py
@@ -20,7 +20,7 @@
 
 
 def kernel(nz, chunks, hc, piece, sel, q_in, k_in, v_in, hk_in, hv_in, w_in, out,
-           qx, kb, vb, hkb, hvb, hkw, hvw, ocs, mls, ocr, mlr, r, rml, zlb, zlml, zrb, zrml, fs, att, bias,
+           qx, kb, vb, hkb, hvb, hkw, hvw, ocs, mls, ocr, mlr, r, rml, zlb, zlml, zrb, zrml, fs, att, bias, vt,
            wbuf, acc, ysend, yrecv,
            q_loc, q_xs, q_xr, kv_loc, kv_xs, kv_xr,
            qc_s, qc_r, qr_s, qr_r, ql_s, ql_r,
@@ -139,24 +139,32 @@
         lanes = slice(h * HDIM, (h + 1) * HDIM)
         qs = qx[t * 2 + cc, k, :, :, lanes].reshape(both, HDIM)
         kc = kb[k, :, :, lanes].reshape(both, HDIM)
-        vc = vb[k, :, :, lanes].reshape(both, HDIM)
-        kh, vh = [], []
+        mid, lane_half = both // 2 // HDIM * HDIM, both // 2 // HDIM * HDIM + HDIM
+        spans = (slice(0, lane_half), slice(mid, both))
+        s1 = lax.dot_general(kc, qs, NT, preferred_element_type=F32)
+        values, scores = [], []
         for xx in range(2):
             b = t * PLANE + xx * 2 + cc
-            for src in range(2):
-                for slot in range(CAP):
-                    n = sel[b, src * 4 + slot]
-                    kh.append(hkw[src, n, :, lanes])
-                    vh.append(hvw[src, n, :, lanes])
-        kh, vh = jnp.concatenate(kh, axis=0), jnp.concatenate(vh, axis=0)
-        s1 = lax.dot_general(kc, qs, NT, preferred_element_type=F32)
-        s2 = lax.dot_general(kh, qs, NT, preferred_element_type=F32) + bias[t * 2 + cc]
-        m = jnp.maximum(jnp.max(s1, axis=0, keepdims=True), jnp.max(s2, axis=0, keepdims=True))
+            picks = [(src, sel[b, src * 4 + slot]) for src in range(2) for slot in range(CAP)]
+            kh = jnp.concatenate([hkw[src, n, :, lanes] for src, n in picks], axis=0)
+            values.append(jnp.concatenate([hvw[src, n, :, lanes] for src, n in picks], axis=0))
+            score = lax.dot_general(kh, qs[spans[xx]], NT, preferred_element_type=F32)
+            scores.append(score + bias[t * 2 + cc, xx])
+
+        def joined(op, cur, first, last):
+            return jnp.concatenate([
+                op(cur[:, :mid], first[:, :mid]),
+                op(op(cur[:, mid:lane_half], first[:, mid:]), last[:, :HDIM]),
+                op(cur[:, lane_half:], last[:, HDIM:])], axis=1)
+
+        m = joined(jnp.maximum, jnp.max(s1, axis=0, keepdims=True),
+                   *[jnp.max(score, axis=0, keepdims=True) for score in scores])
         p1 = jnp.exp2((s1 - m) * LOG2)
-        p2 = jnp.exp2((s2 - m) * LOG2)
-        l = jnp.sum(p1, axis=0, keepdims=True) + jnp.sum(p2, axis=0, keepdims=True)
-        o = lax.dot_general(vc, p1.astype(BF16), TN, preferred_element_type=F32)
-        o = o + lax.dot_general(vh, p2.astype(BF16), TN, preferred_element_type=F32)
+        ph = [jnp.exp2((score - m[:, span]) * LOG2) for score, span in zip(scores, spans)]
+        cur = jnp.dot(vt[h], p1.astype(BF16), preferred_element_type=F32)
+        l = joined(jnp.add, cur[HDIM:HDIM + 1], *[jnp.sum(p, axis=0, keepdims=True) for p in ph])
+        o = joined(jnp.add, cur[:HDIM], *[
+            lax.dot_general(v, p.astype(BF16), TN, preferred_element_type=F32) for v, p in zip(values, ph)])
         return o, m, l
 
     def rs_step(k, wave):
@@ -267,26 +275,33 @@
     pl.semaphore_wait(barrier, 3 + has_left.astype(jnp.int32) + has_right.astype(jnp.int32))
 
     for k in range(chunks):
+        q_own(k).start()
+    for k in range(min(nz + 1, chunks)):
         q_cross(k).start()
-        q_own(k).start()
-    for k in range(min(2, chunks)):
-        kv_start(k)
+    kv_start(0)
+    for k in range(nz + 1, chunks):
+        q_cross(k).start()
+    if chunks > 1:
+        kv_start(1)
     for k in range(min(2, chunks)):
         for side in range(2):
             w_fetch(k, side).start()
     acc[...] = jnp.zeros_like(acc)
-
-    block_of = lax.broadcasted_iota(jnp.int32, (piece, both), 1) // tok
+    vt[...] = jnp.ones_like(vt)
+
+    mid = both // 2 // HDIM * HDIM
+    lane = lax.broadcasted_iota(jnp.int32, (piece, mid + HDIM), 1)
 
     def fill(i, _):
         t, cc = i // 2, i % 2
         for xx in range(2):
             b = t * PLANE + xx * 2 + cc
+            inside = lane >= tok - mid if xx else lane < tok
             for src in range(2):
                 for slot in range(CAP):
-                    n = (xx * 2 + src) * CAP + slot
+                    n = src * CAP + slot
                     live = (sel[b, src * 4 + CAP + slot].astype(F32) - 1.0) * 1e30
-                    bias[i, n * piece:(n + 1) * piece, :] = jnp.where(block_of == xx, live, -1e30)
+                    bias[i, xx, n * piece:(n + 1) * piece, :] = jnp.where(inside, live, -1e30)
         return 0
 
     lax.fori_loop(0, nz * 2, fill, 0)
@@ -318,6 +333,8 @@
                 @pl.when(k + nz - d < chunks)
                 def _():
                     q_forward(k + nz - d, d)
+            for h in range(hc):
+                vt[h, :HDIM, :] = jnp.transpose(vb[k, :, :, h * HDIM:(h + 1) * HDIM].reshape(both, HDIM))
             hkw[...] = hkb[k].reshape(hkw.shape)
             hvw[...] = hvb[k].reshape(hvw.shape)
 
@@ -459,7 +476,8 @@
         vm((2, hist // piece, piece, w), BF16), vm((2, hist // piece, piece, w), BF16),
         o_buf, ml_buf, o_buf, ml_buf, o_buf, ml_buf, o_buf, ml_buf, o_buf, ml_buf,
         vm((chunks, tok, w), BF16), vm((2, chunks, tok, w), BF16),
-        vm((nz * 2, 4 * CAP * piece, both), F32),
+        vm((nz * 2, 2, 2 * CAP * piece, both // 2 // HDIM * HDIM + HDIM), F32),
+        vm((hc, HDIM + 16, both), BF16),
         vm((2, 2, w, out_width), BF16), vm((tok, out_width), F32),
         vm((tiles, tok, tile), BF16), vm((tiles, tok, tile), BF16),
     ]
@@ -571,6 +589,7 @@
     def run(*args):
         heads = args[0].shape[1] // mesh.shape["head"] // HDIM
         whole_planes = mesh.shape["seq"] % PLANE == 0 and heads % 2 == 0 and mesh.shape["head"] == 2
+        whole_planes = whole_planes and args[0].shape[0] // mesh.shape["seq"] % HDIM == HDIM // 2
         return jax.shard_map(
             local_fused if whole_planes else local,
             mesh=mesh, in_specs=placed, out_specs=P("seq", "head"), check_vma=False,

time: 172 us -> 170 us (0.988)
  no operation moved by 1% of the time
where the time goes in v3:
time: 170 us
  Pallas kernels  162 us (95%)
  local copies, waits for them, and re-layouts  3.3 us (2%)
  starting transfers between devices  2.94 us (2%)
    pallas_call x1, Pallas kernels, local_fused(): pl.pallas_call(functools.partial(kernel, nz, chunks, hc, piece), out_shap...  162 us
  transfers between devices with their start and end apart: 1, of which 1 were waited for; matrix products, arithmetic and copies ran while one was open for 0% of the time, Pallas kernels for 0%

profile of v3, /device:TPU:0, one launch (start us, length us, event | category | flops | bytes accessed | tf_op | source)
XLA Modules:
  0.0 170.2 jit_solution(7193718240678746706)
XLA Ops:
  0.0 0.8 fusion
  0.8 0.1 copy.23
  0.9 2.9 %collective-permute-start = (s32[16,4]{1,0:T(8,128)S(1)}, s32[16,4]{1,0:T(8,128)S(1)}, u32[]{:S(2)}, u32[]{:S(2)}) collective-permute-start(s32[16,4]{1,0:T(8,128)S(1)} %copy.23), channel_id=1, source_target_pairs={{0,4},{2,6},{4,0},{6,2},{8,12},{10,14},{12,8},{14,10},{16,20},{18,... | collective-permute-start | bytes 776 | tf_op jit(solution)/shard_map/ppermute | solution.py:466
  3.9 0.1 copy.24
  4.0 0.1 copy.25
  4.0 0.1 copy.26
  4.1 0.1 copy.27
  4.2 1.3 collective-permute-done
  5.5 0.7 concatenate.4.sel
  6.2 161.8 %shard_map.73 = bf16[192,2560]{1,0:T(8,128)(2,1)} custom-call(s32[16,8]{1,0:T(8,128)} %concatenate.4.sel, bf16[192,2560]{1,0:T(8,128)(2,1)} %q_in.1, bf16[192,2560]{1,0:T(8,128)(2,1)} %k_in.1, bf16[192,2560]{1,0:T(8,128)(2,1)} %v_in.1, bf16[448,2560]{1,0:T(8,128)(2,1)} %hk_in.1, bf16[448,2560]{1,0:T(8,128)(2,1)} %hv_in.1, bf16[2560,5120]{1,0:T(8,128)(2,1)} %w_in.1), custom_call_target="tpu_custom_call" | custom-call | flops 10066329600 | bytes 5898240 | tf_op jit(solution)/shard_map/pallas_call | solution.py:488
  167.9 2.2 %copy.29 = bf16[192,2560]{1,0:T(8,128)(2,1)} copy(bf16[192,2560]{1,0:T(8,128)(2,1)} %shard_map.73) | data formatting | bytes 1966080
  (5 shorter events, 0.1 us)
Async XLA Ops:
  0.9 4.6 %collective-permute-start = (s32[16,4]{1,0:T(8,128)S(1)}, s32[16,4]{1,0:T(8,128)S(1)}, u32[]{:S(2)}, u32[]{:S(2)}) collective-permute-start(s32[16,4]{1,0:T(8,128)S(1)} %copy.23), channel_id=1, source_target_pairs={{0,4},{2,6},{4,0},{6,2},{8,12},{10,14},{12,8},{14,10},{16,20},{18,... | collective-permute-start | bytes 776 | tf_op jit(solution)/shard_map/ppermute | solution.py:466

commit v4 on v3

--- a/solution.py
+++ b/solution.py
@@ -21,11 +21,11 @@
 
 def kernel(nz, chunks, hc, piece, sel, q_in, k_in, v_in, hk_in, hv_in, w_in, out,
            qx, kb, vb, hkb, hvb, hkw, hvw, ocs, mls, ocr, mlr, r, rml, zlb, zlml, zrb, zrml, fs, att, bias, vt,
-           wbuf, acc, ysend, yrecv,
+           wbuf, acc, ysend, yrecv, wy, atty,
            q_loc, q_xs, q_xr, kv_loc, kv_xs, kv_xr,
            qc_s, qc_r, qr_s, qr_r, ql_s, ql_r,
            oc_s, oc_r, om_s, om_r, zl_s, zl_r, zlm_s, zlm_r, zr_s, zr_r, zrm_s, zrm_r,
-           w_sem, f_s, f_r, y_s, y_r):
+           w_sem, f_s, f_r, y_s, y_r, wy_s, wy_r, ay_s, ay_r):
     s = lax.axis_index("seq")
     hd = lax.axis_index("head")
     z, x, c = s // PLANE, (s // 2) % 2, s % 2
@@ -39,6 +39,8 @@
     right = (jnp.minimum(s + PLANE, nz * PLANE - 1), hd)
     yp = (s, 1 - hd)
     tiles, _, tile = ysend.shape
+    late = wy.shape[0]
+    early = chunks - late
     has_left, has_right = z > 0, z < nz - 1
     own = z * 2 + c
 
@@ -212,8 +214,21 @@
     def y_cross(i):
         return remote(ysend.at[i], yrecv.at[i], y_s.at[i], y_r.at[i], yp)
 
+    def wy_cross(g, side):
+        rows = pl.ds(pl.multiple_of(side * half + (early + g) * w, HDIM), w)
+        lanes = pl.ds(pl.multiple_of((1 - hd) * tiles * tile, tile), tiles * tile)
+        return remote(w_in.at[rows, lanes], wy.at[g, side], wy_s.at[g, side], wy_r.at[g, side], yp)
+
+    def atty_cross(g):
+        return remote(att.at[:, early + g], atty.at[g], ay_s.at[g], ay_r.at[g], yp)
+
     def project(k):
         final_cross(k).wait_recv()
+
+        @pl.when(k >= early)
+        def _():
+            atty_cross(k - early).start()
+
         for side in range(2):
             w_fetch(k, side).wait()
         a = jnp.concatenate([att[0, k], att[1, k]], axis=1)
@@ -224,17 +239,32 @@
             value = acc[:, lanes] + jnp.dot(a, b, preferred_element_type=F32)
             acc[:, lanes] = value
 
-            @pl.when((k == chunks - 1) & (i < tiles))
+            @pl.when((k == early - 1) & (i < tiles))
             def _():
                 ysend[i] = value.astype(BF16)
                 y_cross(i).start()
             return 0
-        lax.fori_loop(0, 2 * tiles, one, 0)
+        lax.fori_loop(jnp.where(k < early, 0, tiles), 2 * tiles, one, 0)
 
         @pl.when(k + 2 < chunks)
         def _():
             for side in range(2):
                 w_fetch(k + 2, side).start()
+
+        @pl.when(k >= early)
+        def _():
+            g = k - early
+            for side in range(2):
+                wy_cross(g, side).wait_recv()
+            atty_cross(g).wait_recv()
+            a = jnp.concatenate([atty[g, 0], atty[g, 1]], axis=1)
+
+            def one(i, _):
+                lanes = pl.ds(pl.multiple_of((hd * tiles + i) * tile, tile), tile)
+                b = wy[g, :, :, pl.ds(pl.multiple_of(i * tile, tile), tile)].reshape(2 * w, tile)
+                acc[:, lanes] += jnp.dot(a, b, preferred_element_type=F32)
+                return 0
+            lax.fori_loop(0, tiles, one, 0)
 
     def final(k):
         @pl.when(has_left)
@@ -283,6 +313,9 @@
         q_cross(k).start()
     if chunks > 1:
         kv_start(1)
+    for g in range(late):
+        for side in range(2):
+            wy_cross(g, side).start()
     for k in range(min(2, chunks)):
         for side in range(2):
             w_fetch(k, side).start()
@@ -306,11 +339,18 @@
 
     lax.fori_loop(0, nz * 2, fill, 0)
 
+    ahead = [2 * (nz - d) - 1 for d in range(nz)]
+    ahead[0] = 2 * nz
     for k in range(min(nz + 1, chunks)):
         q_hop1(k)
-    for k in range(min(nz - 1, chunks)):
-        for d in range(1, nz - k):
-            q_forward(k, d)
+    for d in range(1, nz):
+        q_forward(0, d)
+    for k in range(min(nz + 1, chunks), min(ahead[0], chunks)):
+        q_hop1(k)
+    for k in range(1, chunks):
+        for d in range(1, nz):
+            if k < ahead[d]:
+                q_forward(k, d)
 
     def slot_body(j, _):
         k, second = j // 2, j % 2
@@ -325,14 +365,14 @@
             def _():
                 kv_start(k + 2)
 
-            @pl.when(k + nz + 1 < chunks)
-            def _():
-                q_hop1(k + nz + 1)
+            @pl.when(k + ahead[0] < chunks)
+            def _():
+                q_hop1(k + ahead[0])
 
             for d in range(1, nz):
-                @pl.when(k + nz - d < chunks)
+                @pl.when(k + ahead[d] < chunks)
                 def _():
-                    q_forward(k + nz - d, d)
+                    q_forward(k + ahead[d], d)
             for h in range(hc):
                 vt[h, :HDIM, :] = jnp.transpose(vb[k, :, :, h * HDIM:(h + 1) * HDIM].reshape(both, HDIM))
             hkw[...] = hkb[k].reshape(hkw.shape)
@@ -402,6 +442,10 @@
         return 0
 
     lax.fori_loop(0, tiles, finish, 0)
+    for g in range(late):
+        atty_cross(g).wait_send()
+        for side in range(2):
+            wy_cross(g, side).wait_send()
 
     def drain(k, _):
         q_cross(k).wait_send()
@@ -458,6 +502,7 @@
     out_width = out_weight.shape[1]
     tile = 512 if out_width % 1024 == 0 else HDIM
     tiles = out_width // 2 // tile
+    late = 2
     chunks = half_heads // hc
     w = hc * HDIM
     both = 2 * tok
@@ -480,9 +525,11 @@
         vm((hc, HDIM + 16, both), BF16),
         vm((2, 2, w, out_width), BF16), vm((tok, out_width), F32),
         vm((tiles, tok, tile), BF16), vm((tiles, tok, tile), BF16),
+        vm((late, 2, w, out_width // 2), BF16), vm((late, 2, tok, w), BF16),
     ]
     scratch += [sem((chunks,))] * 3 + [sem((4, chunks))] * 3 + [sem((nz, chunks))] * 18
     scratch += [sem((2, chunks))] + [sem((chunks,))] * 2 + [sem((tiles,))] * 2
+    scratch += [sem((late, 2))] * 2 + [sem((late,))] * 2
     any_spec = pl.BlockSpec(memory_space=pl.ANY)
     flops = 4 * readers * tok * (2 * tok + 4 * CAP * piece) * width // 2
     return pl.pallas_call(
@@ -588,7 +635,7 @@
 
     def run(*args):
         heads = args[0].shape[1] // mesh.shape["head"] // HDIM
-        whole_planes = mesh.shape["seq"] % PLANE == 0 and heads % 2 == 0 and mesh.shape["head"] == 2
+        whole_planes = mesh.shape["seq"] % PLANE == 0 and heads % 2 == 0 and heads > 4 and mesh.shape["head"] == 2
         whole_planes = whole_planes and args[0].shape[0] // mesh.shape["seq"] % HDIM == HDIM // 2
         return jax.shard_map(
             local_fused if whole_planes else local,

time: 170 us -> 177 us (1.041)
  Pallas kernels: 162 us -> 168 us
    pallas_call x1, Pallas kernels: 162 us -> 168 us  [local_fused(): pl.pallas_call(functools.partial(kernel, nz, chunks, hc, piece), out_shap...]
where the time goes in v4:
time: 177 us; the launch traced here: 176 us
  Pallas kernels  168 us (95%)
  local copies, waits for them, and re-layouts  3.3 us (2%)
  starting transfers between devices  2.94 us (2%)
    pallas_call x1, Pallas kernels, local_fused(): pl.pallas_call(functools.partial(kernel, nz, chunks, hc, piece), out_shap...  168 us
  transfers between devices with their start and end apart: 1, of which 1 were waited for; matrix products, arithmetic and copies ran while one was open for 0% of the time, Pallas kernels for 0%

profile of v4, /device:TPU:0, one launch (start us, length us, event | category | flops | bytes accessed | tf_op | source)
XLA Modules:
  0.0 176.3 jit_solution(18112229243249173034)
XLA Ops:
  0.0 0.8 fusion
  0.8 0.1 copy.23
  0.9 2.9 %collective-permute-start = (s32[16,4]{1,0:T(8,128)S(1)}, s32[16,4]{1,0:T(8,128)S(1)}, u32[]{:S(2)}, u32[]{:S(2)}) collective-permute-start(s32[16,4]{1,0:T(8,128)S(1)} %copy.23), channel_id=1, source_target_pairs={{0,4},{2,6},{4,0},{6,2},{8,12},{10,14},{12,8},{14,10},{16,20},{18,... | collective-permute-start | bytes 776 | tf_op jit(solution)/shard_map/ppermute | solution.py:511
  3.9 0.1 copy.24
  4.0 0.1 copy.25
  4.0 0.1 copy.26
  4.1 0.1 copy.27
  4.2 1.3 collective-permute-done
  5.5 0.7 concatenate.4.sel
  6.2 167.9 %shard_map.73 = bf16[192,2560]{1,0:T(8,128)(2,1)} custom-call(s32[16,8]{1,0:T(8,128)} %concatenate.4.sel, bf16[192,2560]{1,0:T(8,128)(2,1)} %q_in.1, bf16[192,2560]{1,0:T(8,128)(2,1)} %k_in.1, bf16[192,2560]{1,0:T(8,128)(2,1)} %v_in.1, bf16[448,2560]{1,0:T(8,128)(2,1)} %hk_in.1, bf16[448,2560]{1,0:T(8,128)(2,1)} %hv_in.1, bf16[2560,5120]{1,0:T(8,128)(2,1)} %w_in.1), custom_call_target="tpu_custom_call" | custom-call | flops 10066329600 | bytes 5898240 | tf_op jit(solution)/shard_map/pallas_call | solution.py:535
  174.1 2.2 %copy.29 = bf16[192,2560]{1,0:T(8,128)(2,1)} copy(bf16[192,2560]{1,0:T(8,128)(2,1)} %shard_map.73) | data formatting | bytes 1966080
  (5 shorter events, 0.1 us)
Async XLA Ops:
  0.9 4.6 %collective-permute-start = (s32[16,4]{1,0:T(8,128)S(1)}, s32[16,4]{1,0:T(8,128)S(1)}, u32[]{:S(2)}, u32[]{:S(2)}) collective-permute-start(s32[16,4]{1,0:T(8,128)S(1)} %copy.23), channel_id=1, source_target_pairs={{0,4},{2,6},{4,0},{6,2},{8,12},{10,14},{12,8},{14,10},{16,20},{18,... | collective-permute-start | bytes 776 | tf_op jit(solution)/shard_map/ppermute | solution.py:511

commit v5 on v3

--- a/solution.py
+++ b/solution.py
@@ -19,13 +19,14 @@
 TN = (((0,), (0,)), ((), ()))
 
 
-def kernel(nz, chunks, hc, piece, sel, q_in, k_in, v_in, hk_in, hv_in, w_in, out,
+def kernel(nz, chunks, hc, piece, tab_in, q_in, k_in, v_in, hk_in, hv_in, w_in, out,
            qx, kb, vb, hkb, hvb, hkw, hvw, ocs, mls, ocr, mlr, r, rml, zlb, zlml, zrb, zrml, fs, att, bias, vt,
-           wbuf, acc, ysend, yrecv,
+           wbuf, acc, ysend, yrecv, wy, atty,
            q_loc, q_xs, q_xr, kv_loc, kv_xs, kv_xr,
            qc_s, qc_r, qr_s, qr_r, ql_s, ql_r,
            oc_s, oc_r, om_s, om_r, zl_s, zl_r, zlm_s, zlm_r, zr_s, zr_r, zrm_s, zrm_r,
-           w_sem, f_s, f_r, y_s, y_r):
+           w_sem, f_s, f_r, y_s, y_r, wy_s, wy_r, ay_s, ay_r,
+           sel, tab, tab_l, tab_s, tab_r):
     s = lax.axis_index("seq")
     hd = lax.axis_index("head")
     z, x, c = s // PLANE, (s // 2) % 2, s % 2
@@ -39,6 +40,10 @@
     right = (jnp.minimum(s + PLANE, nz * PLANE - 1), hd)
     yp = (s, 1 - hd)
     tiles, _, tile = ysend.shape
+    late = wy.shape[0]
+    early = chunks - late
+    parts = 4
+    pieces = late * 2 * parts
     has_left, has_right = z > 0, z < nz - 1
     own = z * 2 + c
 
@@ -145,7 +150,7 @@
         values, scores = [], []
         for xx in range(2):
             b = t * PLANE + xx * 2 + cc
-            picks = [(src, sel[b, src * 4 + slot]) for src in range(2) for slot in range(CAP)]
+            picks = [(src, sel[src, b, slot]) for src in range(2) for slot in range(CAP)]
             kh = jnp.concatenate([hkw[src, n, :, lanes] for src, n in picks], axis=0)
             values.append(jnp.concatenate([hvw[src, n, :, lanes] for src, n in picks], axis=0))
             score = lax.dot_general(kh, qs[spans[xx]], NT, preferred_element_type=F32)
@@ -212,8 +217,23 @@
     def y_cross(i):
         return remote(ysend.at[i], yrecv.at[i], y_s.at[i], y_r.at[i], yp)
 
+    def wy_cross(n):
+        g, side, part = n // (2 * parts), n // parts % 2, n % parts
+        rows = pl.ds(pl.multiple_of(side * half + (early + g) * w + part * (w // parts), w // parts), w // parts)
+        lanes = pl.ds(pl.multiple_of((1 - hd) * tiles * tile, tile), tiles * tile)
+        into = wy.at[g, side, pl.ds(pl.multiple_of(part * (w // parts), w // parts), w // parts)]
+        return remote(w_in.at[rows, lanes], into, wy_s.at[n], wy_r.at[n], yp)
+
+    def atty_cross(g):
+        return remote(att.at[:, early + g], atty.at[g], ay_s.at[g], ay_r.at[g], yp)
+
     def project(k):
         final_cross(k).wait_recv()
+
+        @pl.when(k >= early)
+        def _():
+            atty_cross(k - early).start()
+
         for side in range(2):
             w_fetch(k, side).wait()
         a = jnp.concatenate([att[0, k], att[1, k]], axis=1)
@@ -224,17 +244,32 @@
             value = acc[:, lanes] + jnp.dot(a, b, preferred_element_type=F32)
             acc[:, lanes] = value
 
-            @pl.when((k == chunks - 1) & (i < tiles))
+            @pl.when((k == early - 1) & (i < tiles))
             def _():
                 ysend[i] = value.astype(BF16)
                 y_cross(i).start()
             return 0
-        lax.fori_loop(0, 2 * tiles, one, 0)
+        lax.fori_loop(jnp.where(k < early, 0, tiles), 2 * tiles, one, 0)
 
         @pl.when(k + 2 < chunks)
         def _():
             for side in range(2):
                 w_fetch(k + 2, side).start()
+
+        @pl.when(k >= early)
+        def _():
+            g = k - early
+            for n in range(2 * parts):
+                wy_cross(g * 2 * parts + n).wait_recv()
+            atty_cross(g).wait_recv()
+            a = jnp.concatenate([atty[g, 0], atty[g, 1]], axis=1)
+
+            def one(i, _):
+                lanes = pl.ds(pl.multiple_of((hd * tiles + i) * tile, tile), tile)
+                b = wy[g, :, :, pl.ds(pl.multiple_of(i * tile, tile), tile)].reshape(2 * w, tile)
+                acc[:, lanes] += jnp.dot(a, b, preferred_element_type=F32)
+                return 0
+            lax.fori_loop(0, tiles, one, 0)
 
     def final(k):
         @pl.when(has_left)
@@ -274,6 +309,10 @@
 
     pl.semaphore_wait(barrier, 3 + has_left.astype(jnp.int32) + has_right.astype(jnp.int32))
 
+    tab_cross = remote(tab_in, tab, tab_s.at[0], tab_r.at[0], xp)
+    tab_cross.start()
+    tab_own = pltpu.make_async_copy(tab_in, sel.at[0], tab_l.at[0])
+    tab_own.start()
     for k in range(chunks):
         q_own(k).start()
     for k in range(min(nz + 1, chunks)):
@@ -300,10 +339,15 @@
             for src in range(2):
                 for slot in range(CAP):
                     n = src * CAP + slot
-                    live = (sel[b, src * 4 + CAP + slot].astype(F32) - 1.0) * 1e30
+                    live = (sel[src, b, CAP + slot].astype(F32) - 1.0) * 1e30
                     bias[i, xx, n * piece:(n + 1) * piece, :] = jnp.where(inside, live, -1e30)
         return 0
 
+    tab_own.wait()
+    tab_cross.wait()
+    tab_other = pltpu.make_async_copy(tab, sel.at[1], tab_l.at[1])
+    tab_other.start()
+    tab_other.wait()
     lax.fori_loop(0, nz * 2, fill, 0)
 
     for k in range(min(nz + 1, chunks)):
@@ -314,6 +358,10 @@
 
     def slot_body(j, _):
         k, second = j // 2, j % 2
+
+        @pl.when((j >= 1) & (j <= pieces))
+        def _():
+            wy_cross(j - 1).start()
 
         @pl.when((k < chunks) & (second == 0))
         def _():
@@ -402,6 +450,10 @@
         return 0
 
     lax.fori_loop(0, tiles, finish, 0)
+    for g in range(late):
+        atty_cross(g).wait_send()
+    for n in range(pieces):
+        wy_cross(n).wait_send()
 
     def drain(k, _):
         q_cross(k).wait_send()
@@ -458,13 +510,13 @@
     out_width = out_weight.shape[1]
     tile = 512 if out_width % 1024 == 0 else HDIM
     tiles = out_width // 2 // tile
+    late = 2
     chunks = half_heads // hc
     w = hc * HDIM
     both = 2 * tok
     piece = hist // piece_readers.shape[0]
     table = reader_table(piece_readers, readers)
-    other = lax.ppermute(table, "seq", [(i, i ^ 2) for i in range(readers)])
-    sel = jnp.concatenate([table, other], axis=1)
+    table = jnp.pad(table, ((0, 0), (0, HDIM - table.shape[1])))
     vm = pltpu.VMEM
     sem = pltpu.SemaphoreType.DMA
     o_buf = vm((nz, chunks, w, both), BF16)
@@ -480,21 +532,24 @@
         vm((hc, HDIM + 16, both), BF16),
         vm((2, 2, w, out_width), BF16), vm((tok, out_width), F32),
         vm((tiles, tok, tile), BF16), vm((tiles, tok, tile), BF16),
+        vm((late, 2, w, out_width // 2), BF16), vm((late, 2, tok, w), BF16),
     ]
     scratch += [sem((chunks,))] * 3 + [sem((4, chunks))] * 3 + [sem((nz, chunks))] * 18
     scratch += [sem((2, chunks))] + [sem((chunks,))] * 2 + [sem((tiles,))] * 2
+    scratch += [sem((late * 8,))] * 2 + [sem((late,))] * 2
+    scratch += [pltpu.SMEM((2, readers, HDIM), jnp.int32), vm((readers, HDIM), jnp.int32), sem((2,)), sem((1,)), sem((1,))]
     any_spec = pl.BlockSpec(memory_space=pl.ANY)
     flops = 4 * readers * tok * (2 * tok + 4 * CAP * piece) * width // 2
     return pl.pallas_call(
         functools.partial(kernel, nz, chunks, hc, piece),
         out_shape=jax.ShapeDtypeStruct((tok, out_width // 2), BF16),
-        in_specs=[pl.BlockSpec(memory_space=pltpu.SMEM)] + [any_spec] * 6,
+        in_specs=[any_spec] * 7,
         out_specs=pl.BlockSpec(memory_space=pltpu.VMEM),
         scratch_shapes=scratch,
         compiler_params=pltpu.CompilerParams(
             collective_id=0, has_side_effects=True, vmem_limit_bytes=62 * 1024 * 1024),
         cost_estimate=pl.CostEstimate(flops=flops, bytes_accessed=12 * tok * width, transcendentals=flops // 512),
-    )(sel, queries, cur_keys, cur_values, hist_keys, hist_values, out_weight)
+    )(table, queries, cur_keys, cur_values, hist_keys, hist_values, out_weight)
 
 
 def passed_along(value, axis, by):
@@ -588,7 +643,7 @@
 
     def run(*args):
         heads = args[0].shape[1] // mesh.shape["head"] // HDIM
-        whole_planes = mesh.shape["seq"] % PLANE == 0 and heads % 2 == 0 and mesh.shape["head"] == 2
+        whole_planes = mesh.shape["seq"] % PLANE == 0 and heads % 2 == 0 and heads > 4 and mesh.shape["head"] == 2
         whole_planes = whole_planes and args[0].shape[0] // mesh.shape["seq"] % HDIM == HDIM // 2
         return jax.shard_map(
             local_fused if whole_planes else local,

time: 170 us -> 167 us (0.982)
  starting transfers between devices: 2.94 us -> 0 us
    ppermute x1 -> x0, starting transfers between devices: 2.94 us -> none  [local_fused(): other = lax.ppermute(table, 'seq', [(i, i ^ 2) for i in range(readers)])]
  transfers between devices with their start and end apart: 1 -> 0, of which waited for: 1 -> 0; matrix products, arithmetic and copies ran while one was open for 0% -> 0% of each run, Pallas kernels for 0% -> 0%
where the time goes in v5:
time: 167 us
  Pallas kernels  163 us (98%)
  local copies, waits for them, and re-layouts  2.9 us (2%)
    pallas_call x1, Pallas kernels, local_fused(): pl.pallas_call(functools.partial(kernel, nz, chunks, hc, piece), out_shap...  163 us

profile of v5, /device:TPU:0, one launch (start us, length us, event | category | flops | bytes accessed | tf_op | source)
XLA Modules:
  0.0 166.7 jit_solution(7198497039108808749)
XLA Ops:
  0.0 0.8 fusion
  0.8 0.1 copy.15
  0.9 0.6 pad.4.tab_in
  1.5 162.9 %shard_map.73 = bf16[192,2560]{1,0:T(8,128)(2,1)} custom-call(s32[16,128]{1,0:T(8,128)} %pad.4.tab_in, bf16[192,2560]{1,0:T(8,128)(2,1)} %q_in.1, bf16[192,2560]{1,0:T(8,128)(2,1)} %k_in.1, bf16[192,2560]{1,0:T(8,128)(2,1)} %v_in.1, bf16[448,2560]{1,0:T(8,128)(2,1)} %hk_in.1, bf16[448,2560]{1,0:T(8,128)(2,1)} %hv_in.1, bf16[2560,5120]{1,0:T(8,128)(2,1)} %w_in.1), custom_call_target="tpu_custom_call" | custom-call | flops 10066329600 | bytes 5898240 | tf_op jit(solution)/shard_map/pallas_call | solution.py:543
  164.5 2.2 %copy.17 = bf16[192,2560]{1,0:T(8,128)(2,1)} copy(bf16[192,2560]{1,0:T(8,128)(2,1)} %shard_map.73) | data formatting | bytes 1966080
  (5 shorter events, 0.1 us)

commit v6 on v5

--- a/solution.py
+++ b/solution.py
@@ -510,7 +510,7 @@
     out_width = out_weight.shape[1]
     tile = 512 if out_width % 1024 == 0 else HDIM
     tiles = out_width // 2 // tile
-    late = 2
+    late = 1
     chunks = half_heads // hc
     w = hc * HDIM
     both = 2 * tok

time: 167 us -> 165 us (0.988)
  Pallas kernels: 163 us -> 161 us
    pallas_call x1, Pallas kernels: 163 us -> 161 us  [local_fused(): pl.pallas_call(functools.partial(kernel, nz, chunks, hc, piece), out_shap...]
where the time goes in v6:
time: 165 us; the launch traced here: 164 us
  Pallas kernels  161 us (98%)
  local copies, waits for them, and re-layouts  2.9 us (2%)
    pallas_call x1, Pallas kernels, local_fused(): pl.pallas_call(functools.partial(kernel, nz, chunks, hc, piece), out_shap...  161 us

profile of v6, /device:TPU:0, one launch (start us, length us, event | category | flops | bytes accessed | tf_op | source)
XLA Modules:
  0.0 164.4 jit_solution(14575841946191077887)
XLA Ops:
  0.0 0.8 fusion
  0.8 0.1 copy.15
  0.9 0.6 pad.4.tab_in
  1.5 160.7 %shard_map.73 = bf16[192,2560]{1,0:T(8,128)(2,1)} custom-call(s32[16,128]{1,0:T(8,128)} %pad.4.tab_in, bf16[192,2560]{1,0:T(8,128)(2,1)} %q_in.1, bf16[192,2560]{1,0:T(8,128)(2,1)} %k_in.1, bf16[192,2560]{1,0:T(8,128)(2,1)} %v_in.1, bf16[448,2560]{1,0:T(8,128)(2,1)} %hk_in.1, bf16[448,2560]{1,0:T(8,128)(2,1)} %hv_in.1, bf16[2560,5120]{1,0:T(8,128)(2,1)} %w_in.1), custom_call_target="tpu_custom_call" | custom-call | flops 10066329600 | bytes 5898240 | tf_op jit(solution)/shard_map/pallas_call | solution.py:543
  162.2 2.2 %copy.17 = bf16[192,2560]{1,0:T(8,128)(2,1)} copy(bf16[192,2560]{1,0:T(8,128)(2,1)} %shard_map.73) | data formatting | bytes 1966080
  (5 shorter events, 0.1 us)
